TPU v7x, 128 devices: a whole 4x4x4 slice. The times are simulated.
128 devices in a mesh: leaf: 128 (over y, x, z, core).
Axes of the slice: x: 4, y: 4, z: 4, core: 2. Of those that a mesh axis runs over, the one named last changes fastest.
Arguments:
- points: float32 [3, 524288], P(None, 'leaf'), may hold values from 0 to 1
- rhs: float32 [16, 524288], P(None, 'leaf'), may hold values from -6 to 6
- leaf_basis: float32 [32, 524288], P(None, 'leaf'), may hold values from -0.75 to 0.75
- transfer: float32 [32, 32, 10752], P(None, None, 'leaf'), may hold values from -0.5 to 0.5
- proxies: float32 [3, 32, 10880], P(None, None, 'leaf'), may hold values from 0 to 1
- near_list: int32 [8192, 5], P('leaf'), may hold values from -1 to 8191, as said below
- couple_list: int32 [10752, 20], P('leaf'), may hold values from -1 to 8191, as said below
- root_list: int32 [128, 128], P('leaf'), may hold values from -1 to 127, as said below
Outputs:
- product: float32 [16, 524288], P(None, 'leaf')
Inputs may be any that keep to these rules, and one draw needn't show every extreme that they name: `near_list`: entry [t, j] is the leaf t + j - 2 if the block of leaves t and t + j - 2 is near, else -1; every leaf is near itself. Nearness is defined level by level: at level 0 roots t and s are near when they differ by at most a per-root reach of 1 to 2 (the larger of the two); below, two clusters are near when their parents are near and they differ by at most the larger of their reaches. Near leaf blocks, with the coupled pairs of the other two lists, cover every pair of points exactly once. `couple_list`: the row of a cluster t of level l lists in slot j the cluster s = 4 * (t // 4 - 2) + j of level l if s exists, the parents of t and s are near and t and s are not near, else -1. `root_list`: entry [t, s] is s if roots t and s are not near, else -1.
All inputs are finite; a program needn't handle non-finite values.
Results may differ from a plain program's by a relative error of at most 0.0003.
Values sent between devices are 32-bit elements; how exact they have to be, the bound alone decides.
A program may use at most 128 MiB of HBM per device.

v0:
```python
import math

import jax
import jax.numpy as jnp
from jax import lax
from jax.sharding import PartitionSpec as P

LEAF = 64
LEVELS = 3
REACH = 2
HALO = 11
LEAF_DEV = 64


kernel_band = 0.1
highest = lax.Precision.HIGHEST


def with_halo_2(cells, sides, width):
    for axis, dim in sides:
        count = lax.axis_size(axis)
        ends = count - 1
        head = lax.slice_in_dim(cells, 0, width, axis=dim)
        tail = lax.slice_in_dim(cells, cells.shape[dim] - width, cells.shape[dim], axis=dim)
        cells = jnp.concatenate(
            [
                lax.ppermute(tail, axis, [(i, (i + 1) % count) for i in range(ends)]),
                cells,
                lax.ppermute(head, axis, [((i + 1) % count, i) for i in range(ends)]),
            ],
            axis=dim,
        )
    return cells


def kernel_sq(left_pts, right_pts):
    length = (
        (left_pts[0] - right_pts[0]) ** 2
        + (left_pts[1] - right_pts[1]) ** 2
        + (left_pts[2] - right_pts[2]) ** 2
    )
    return jnp.exp(-length / kernel_band)


def by_blocks(method, inputs, length, stride, out_shape):
    stride = math.gcd(length, stride)

    def advance(step_no, accumulated):
        pieces = [operand for operand in inputs]
        return method(*pieces)

    return lax.fori_loop(0, length // stride, advance, jnp.zeros(out_shape, jnp.float32))


def couple(target_prox, lookup, source_prox, listed):
    usable = listed.T >= 0
    clipped = jnp.where(usable, listed.T, 0)

    def one_block(target_blk, clipped_blk, usable_blk):
        coeff_blk = jnp.take(lookup, clipped_blk, axis=2)
        prox_blk = jnp.take(source_prox, clipped_blk, axis=2)
        kernel = kernel_sq(
            target_blk[:, :, None, None, :], prox_blk[:, None, :, :, :]
        ) * usable_blk.astype(coeff_blk.dtype)
        return jnp.einsum("absn,bksn->akn", kernel, coeff_blk, precision=highest)

    extent = listed.shape[0]
    return by_blocks(
        one_block,
        [target_prox, clipped, usable],
        extent,
        128,
        (lookup.shape[0], lookup.shape[1], extent),
    )


def near_local(targets, lookup, listed, vectors):
    leaves = targets.shape[1]
    total = jnp.zeros((vectors, leaves, targets.shape[2]), jnp.float32)
    for slot_no in range(listed.shape[1]):
        window = lookup[:, slot_no : slot_no + leaves]
        usable = (listed[:, slot_no] >= 0).astype(jnp.float32)
        kernel = (
            kernel_sq(targets[:, :, :, None], window[vectors:, :, None, :]) * usable[:, None, None]
        )
        total = total + jnp.einsum("nij,knj->kni", kernel, window[:vectors], precision=highest)
    return total


def body(points, rhs, leaf_basis, transfer, proxies, near_list, couple_list, root_list):
    device = lax.axis_index("leaf")
    rank_dim = leaf_basis.shape[0]
    vectors = rhs.shape[0]
    leaves = LEAF_DEV
    basis_grid = leaf_basis.reshape(rank_dim, leaves, LEAF)
    coeffs = [None] * (LEVELS + 1)
    coeffs[LEVELS] = jnp.einsum(
        "rnp,knp->rkn", basis_grid, rhs.reshape(vectors, leaves, LEAF), precision=highest
    )
    level_prox = []
    mappings = [None]
    entries = [None]
    for level_no in range(LEVELS + 1):
        extent = 4**level_no
        begin_at = (extent - 1) // 3
        level_prox.append(proxies[:, :, begin_at : begin_at + extent])
        if level_no > 0:
            mappings.append(transfer[:, :, begin_at - 1 : begin_at - 1 + extent])
            entries.append(couple_list[begin_at - 1 : begin_at - 1 + extent])
    for level_no in range(LEVELS, 0, -1):
        merged = jnp.einsum("abn,akn->bkn", mappings[level_no], coeffs[level_no], precision=highest)
        coeffs[level_no - 1] = merged.reshape(rank_dim, vectors, -1, 4).sum(axis=3)
    top_count = 2
    stacked_coeffs = jnp.concatenate([coeffs[level_no] for level_no in range(top_count)], axis=2)
    stacked_prox = jnp.concatenate(level_prox[:top_count], axis=2)
    gathered_coeffs, gathered_prox = (
        lax.all_gather(stacked_coeffs, "leaf", axis=2, tiled=True),
        lax.all_gather(stacked_prox, "leaf", axis=2, tiled=True),
    )
    group = stacked_coeffs.shape[2]
    roots = gathered_coeffs.shape[2] // group
    gathered_coeffs = gathered_coeffs.reshape(rank_dim, vectors, roots, group)
    gathered_prox = gathered_prox.reshape(3, rank_dim, roots, group)
    coupled = []
    for level_no in range(LEVELS + 1):
        extent = 4**level_no
        if level_no < top_count:
            begin_at = (extent - 1) // 3
            lookup = gathered_coeffs[:, :, :, begin_at : begin_at + extent].reshape(
                rank_dim, vectors, roots * extent
            )
            source_prox = gathered_prox[:, :, :, begin_at : begin_at + extent].reshape(
                3, rank_dim, roots * extent
            )
            listed = root_list if level_no == 0 else entries[level_no]
        else:
            joined = jnp.concatenate(
                [
                    coeffs[level_no].reshape(rank_dim * vectors, extent),
                    level_prox[level_no].reshape(3 * rank_dim, extent),
                ],
                axis=0,
            )
            with_rim = with_halo_2(joined, (("leaf", 1),), HALO)
            width_rim = with_rim.shape[1]
            lookup = with_rim[: rank_dim * vectors].reshape(rank_dim, vectors, width_rim)
            source_prox = with_rim[rank_dim * vectors :].reshape(3, rank_dim, width_rim)
            base_index = device * extent - HALO
            listed = jnp.where(entries[level_no] >= 0, entries[level_no] - base_index, -1)
        coupled.append(couple(level_prox[level_no], lookup, source_prox, listed))
    downward = coupled[0]
    for level_no in range(1, LEVELS + 1):
        downward = coupled[level_no] + jnp.einsum(
            "abn,bkn->akn", mappings[level_no], jnp.repeat(downward, 4, axis=2), precision=highest
        )
    joined_pts = jnp.concatenate([rhs, points], axis=0)
    with_halo = with_halo_2(joined_pts, (("leaf", 1),), REACH * LEAF)
    lookup_pts = with_halo.reshape(vectors + 3, leaves + 2 * REACH, LEAF)
    targets = points.reshape(3, leaves, LEAF)
    near_part = near_local(targets, lookup_pts, near_list, vectors)
    far_part = jnp.einsum("rnp,rkn->knp", basis_grid, downward, precision=highest)
    return (near_part + far_part).reshape(vectors, leaves * LEAF)


def solution(mesh):
    in_specs = (
        P(None, "leaf"),
        P(None, "leaf"),
        P(None, "leaf"),
        P(None, None, "leaf"),
        P(None, None, "leaf"),
        P("leaf", None),
        P("leaf", None),
        P("leaf", None),
    )
    out_specs = P(None, "leaf")
    return jax.shard_map(body, mesh=mesh, in_specs=in_specs, out_specs=out_specs, check_vma=False)
```

profile of v0, /device:TPU:0, one launch (start us, length us, event | category | flops | bytes accessed | tf_op | source)
XLA Modules:
  0.0 232.7 jit_solution(15074548665281625737)
XLA Ops:
  6.5 1.0 constant_dynamic-update-slice_fusion.1
  7.5 0.9 constant_dynamic-update-slice_fusion
  9.0 1.3 collective-permute-start.1
  10.3 3.6 %collective-permute-start = (f32[19,128]{1,0:T(8,128)}, f32[19,128]{1,0:T(8,128)}, u32[]{:S(2)}, u32[]{:S(2)}) collective-permute-start(f32[19,128]{1,0:T(8,128)} %get-tuple-element.121), channel_id=1, source_target_pairs={{0,1},{1,2},{2,3},{3,4},{4,5},{5,6},{6,7},{7,8},{8,9},{9,10},{10,1... | collective-permute-start | bytes 29192 | tf_op jit(solution)/shard_map/ppermute | solution.py:27
  14.0 1.1 reshape.369
  15.1 0.9 slice.381
  16.0 1.5 reshape.370
  17.5 2.6 %convolution_bitcast_fusion = f32[32,16,64]{0,1,2:T(8,128)S(1)} fusion(f32[32,64,64]{2,1,0:T(8,128)S(1)} %reshape.370, f32[16,64,64]{2,1,0:T(8,128)S(1)} %reshape.369), kind=kOutput, calls=%fused_computation.140 | convolution fusion | flops 25165824 | bytes 917504 | tf_op jit(solution)/shard_map/rnp,knp->rkn/dot_general | solution.py:97
  20.4 0.9 slice_maximum_fusion
  21.3 1.3 collective-permute-start.3
  22.6 4.3 %collective-permute-start.2 = (f32[608,11]{1,0:T(8,128)}, f32[608,11]{1,0:T(8,128)}, u32[]{:S(2)}, u32[]{:S(2)}) collective-permute-start(f32[608,11]{1,0:T(8,128)} %get-tuple-element.123), channel_id=1, source_target_pairs={{0,1},{1,2},{2,3},{3,4},{4,5},{5,6},{6,7},{7,8},{8,9},{9,10},{10,1... | collective-permute-start | bytes 80264 | tf_op jit(solution)/shard_map/ppermute | solution.py:27
  27.0 1.0 slice.393
  28.1 2.0 copy.172
  30.0 1.0 bitcast_reduce_fusion
  32.1 1.3 collective-permute-start.5
  37.1 50.5 %all_gather.7 = f32[3,32,640]{1,0,2:T(4,128)S(1)} all-gather(f32[3,32,5]{1,0,2:T(4,128)S(1)} %copy.175), channel_id=1, replica_groups=mesh['leaf'=128] {'leaf'}, dimensions={2}, use_global_device_ids=true | all-gather | bytes 247680 | tf_op jit(solution)/shard_map/all_gather | solution.py:118
  92.8 0.8 gather_fusion.7
  103.9 2.5 %collective-permute-start.4 = (f32[608,11]{0,1:T(8,128)}, f32[608,11]{0,1:T(8,128)S(1)}, u32[]{:S(2)}, u32[]{:S(2)}) collective-permute-start(f32[608,11]{0,1:T(8,128)} %get-tuple-element.140), channel_id=1, source_target_pairs={{0,1},{1,2},{2,3},{3,4},{4,5},{5,6},{6,7},{7,8},{8,9},{9,10},{10,1... | collective-permute-start | bytes 80264 | tf_op jit(solution)/shard_map/ppermute | solution.py:27
  106.4 0.8 pad_maximum_fusion
  108.3 6.1 %fusion.48 = f32[64,16,64]{2,1,0:T(8,128)S(1)} fusion(f32[64]{0:T(128)S(1)} %get-tuple-element.150, f32[64,64]{1,0:T(8,128)S(1)} %get-tuple-element.112, f32[64,64]{1,0:T(8,128)S(1)} %get-tuple-element.101, f32[64,64]{1,0:T(8,128)S(1)} %get-tuple-element.90, f32[64,64]{1,0:T(8,128)S(1)} %copy-done.24, f32[64,64]{1,0:T(8,128)S(1)} %copy-done.25, ...), kind=kOutput, calls=%fused_computation.56 | convolution fusion | flops 53215232 | bytes 622848 | tf_op jit(solution)/shard_map/nij,knj->kni/dot_general | solution.py:86
  114.3 6.1 %fusion.74 = f32[64,16,64]{2,1,0:T(8,128)S(1)} fusion(f32[64]{0:T(128)S(1)} %get-tuple-element.147, f32[64,64]{1,0:T(8,128)S(1)} %get-tuple-element.98, f32[64,64]{1,0:T(8,128)S(1)} %get-tuple-element.99, f32[64,64]{1,0:T(8,128)S(1)} %get-tuple-element.100, f32[64,64]{1,0:T(8,128)S(1)} %copy-done.24, f32[64,64]{1,0:T(8,128)S(1)} %copy-done.25, ...), kind=kOutput, calls=%fused_computation.82 | convolution fusion | flops 53215232 | bytes 622848 | tf_op jit(solution)/shard_map/nij,knj->kni/dot_general | solution.py:86
  120.4 6.1 %fusion.87 = f32[64,16,64]{2,1,0:T(8,128)S(1)} fusion(f32[64]{0:T(128)S(1)} %get-tuple-element.148, f32[64,64]{1,0:T(8,128)S(1)} %get-tuple-element.102, f32[64,64]{1,0:T(8,128)S(1)} %get-tuple-element.103, f32[64,64]{1,0:T(8,128)S(1)} %get-tuple-element.104, f32[64,64]{1,0:T(8,128)S(1)} %copy-done.24, f32[64,64]{1,0:T(8,128)S(1)} %copy-done.25, ...), kind=kOutput, calls=%fused_computation.95 | convolution fusion | flops 53215232 | bytes 622848 | tf_op jit(solution)/shard_map/nij,knj->kni/dot_general | solution.py:86
  126.5 6.1 %fusion.138 = f32[64,16,64]{2,1,0:T(8,128)S(1)} fusion(f32[64,16,64]{2,1,0:T(8,128)S(1)} %fusion.74, f32[64,16,64]{2,1,0:T(8,128)S(1)} %fusion.87, f32[64]{0:T(128)S(1)} %get-tuple-element.149, f32[64,64]{1,0:T(8,128)S(1)} %get-tuple-element.114, f32[64,64]{1,0:T(8,128)S(1)} %copy-done.24, f32[64,64]{1,0:T(8,128)S(1)} %get-tuple-element.116, ...), kind=kOutput, calls=%fused_computation.143 | convolution fusion | flops 53346304 | bytes 1147136 | tf_op jit(solution)/shard_map/nij,knj->kni/dot_general | solution.py:86
  132.6 6.0 %fusion.144 = f32[64,16,64]{2,1,0:T(8,128)} fusion(f32[64,16,64]{2,1,0:T(8,128)S(1)} %fusion.48, f32[64,16,64]{2,1,0:T(8,128)S(1)} %fusion.138, f32[64]{0:T(128)S(1)} %get-tuple-element.146, f32[64,64]{1,0:T(8,128)S(1)} %get-tuple-element.88, f32[64,64]{1,0:T(8,128)S(1)} %get-tuple-element.89, f32[64,64]{1,0:T(8,128)S(1)} %get-tuple-element.87, ...), kind=kOutput, calls=%fused_computation.145 | convolution fusion | flops 53346304 | bytes 1147136 | tf_op jit(solution)/shard_map/nij,knj->kni/dot_general | solution.py:86
  138.5 0.9 pad_maximum_fusion.4
  139.6 4.3 %gather_fusion.1 = f32[1280,3,32]{2,1,0:T(4,128)S(1)} fusion(f32[3,32,86]{1,0,2:T(4,128)S(1)} %copy.126, s32[2048]{0:T(1024)S(1)} %pad_clamp_fusion), kind=kCustom, calls=%fused_computation.1 | custom fusion | bytes 988160 | tf_op jit(solution)/shard_map/while/body/eval_jaxpr/jit(_take)/gather | solution.py:61
  143.9 2.6 %copy.162 = f32[20,64,3,32]{1,0,3,2:T(8,128)} copy(f32[20,64,3,32]{3,2,1,0:T(4,128)S(1)} %bitcast.202) | data formatting | bytes 983040 | tf_op jit(solution)/shard_map/while/body/eval_jaxpr/jit(_take)/gather | solution.py:61
  146.5 1.4 select_bitcast_fusion
  148.0 1.3 pad_maximum_fusion.2
  149.3 1.1 copy.132
  150.4 1.1 copy.130
  151.5 1.1 copy.128
  153.0 5.5 %gather_fusion = f32[1280,32,16]{1,2,0:T(8,128)} fusion(f32[32,16,86]{0,1,2:T(8,128)S(1)} %copy.124, s32[2048]{0:T(1024)S(1)} %pad_clamp_fusion), kind=kCustom, calls=%fused_computation | custom fusion | bytes 5248000 | tf_op jit(solution)/shard_map/while/body/eval_jaxpr/jit(_take)/gather | solution.py:60
  159.5 2.0 gather_fusion.3
  161.6 0.8 slice_bitcast_fusion.6
  162.4 0.8 pad_maximum_fusion.3
  163.7 1.9 gather_fusion.2
  165.7 9.4 %fusion.148 = f32[16,16,32]{2,1,0:T(8,128)S(1)} fusion(f32[20,16]{1,0:T(8,128)S(1)} %copy-done.33, f32[32,20,16]{0,2,1:T(8,128)} %get-tuple-element.119, f32[32,16]{0,1:T(8,128)S(1)} %copy-done.34, f32[32,20,16]{0,2,1:T(8,128)} %get-tuple-element.120, f32[32,16]{0,1:T(8,128)S(1)} %copy-done.35, f32[32,20,16]{0,2,1:T(8,128)S(1)} %copy-done.17, ...), kind=kOutput, calls=%fused_computation.149 | convolution fusion | flops 66682880 | bytes 818752 | tf_op jit(solution)/shard_map/while/body/eval_jaxpr/absn,bksn->akn/dot_general | solution.py:65
  175.2 31.6 %fusion.130 = f32[64,16,32]{2,1,0:T(8,128)} fusion(f32[20,64]{1,0:T(8,128)S(1)} %copy-done.32, f32[32,20,64]{0,2,1:T(8,128)S(1)} %copy-done.10, f32[32,64]{0,1:T(8,128)S(1)} %copy-done.21, f32[32,20,64]{0,2,1:T(8,128)S(1)} %copy-done.11, f32[32,64]{0,1:T(8,128)S(1)} %copy-done.22, f32[32,20,64]{0,2,1:T(8,128)S(1)} %copy-done.12, ...), kind=kOutput, calls=%fused_computation.141 | convolution fusion | flops 266731520 | bytes 3275008 | tf_op jit(solution)/shard_map/while/body/eval_jaxpr/absn,bksn->akn/dot_general | solution.py:65
  206.7 4.8 %slice.474 = f32[32,16,128,4]{0,1,3,2:T(8,128)} slice(f32[32,16,128,5]{0,1,3,2:T(8,128)} %bitcast.203), slice={[0:32], [0:16], [0:128], [1:5]} | slice | bytes 2097152 | tf_op jit(solution)/shard_map/slice | solution.py:129
  211.5 1.3 slice_bitcast_fusion
  212.8 2.8 %gather_fusion.4 = f32[80,32,16]{1,2,0:T(8,128)S(1)} fusion(f32[32,16,512]{0,1,2:T(8,128)} %bitcast.200, s32[1024]{0:T(1024)S(1)} %get-tuple-element.153), kind=kCustom, calls=%fused_computation.4 | custom fusion | bytes 328000 | tf_op jit(solution)/shard_map/while/body/eval_jaxpr/jit(_take)/gather | solution.py:60
  215.7 1.0 gather_fusion.6
  217.6 2.1 fusion.153
  219.8 0.8 convolution_bitcast_fusion.1
  221.4 1.7 fusion.129
  223.1 1.6 fusion.128
  224.9 0.9 reshape.390
  (188 shorter events, 26.0 us)
Async XLA Ops:
  6.5 200.2 %all-gather.2.cloned.1.call-start = ((), (), s32[]{:S(2)}) async-start(), calls=%async_computation | async-start | bytes 5283840 | tf_op jit(solution)/shard_map/all_gather | solution.py:117
  8.4 2.0 copy-start.8
  9.0 94.9 %collective-permute-start.1 = (f32[19,128]{1,0:T(8,128)}, f32[19,128]{1,0:T(8,128)}, u32[]{:S(2)}, u32[]{:S(2)}) collective-permute-start(f32[19,128]{1,0:T(8,128)} %get-tuple-element.122), channel_id=1, source_target_pairs={{1,0},{2,1},{3,2},{4,3},{5,4},{6,5},{7,6},{8,7},{9,8},{10,9},{11,1... | collective-permute-start | bytes 29192 | tf_op jit(solution)/shard_map/ppermute | solution.py:29
  10.3 96.1 %collective-permute-start = (f32[19,128]{1,0:T(8,128)}, f32[19,128]{1,0:T(8,128)}, u32[]{:S(2)}, u32[]{:S(2)}) collective-permute-start(f32[19,128]{1,0:T(8,128)} %get-tuple-element.121), channel_id=1, source_target_pairs={{0,1},{1,2},{2,3},{3,4},{4,5},{5,6},{6,7},{7,8},{8,9},{9,10},{10,1... | collective-permute-start | bytes 29192 | tf_op jit(solution)/shard_map/ppermute | solution.py:27
  17.5 10.6 %copy-start = (f32[32,64,64]{2,1,0:T(8,128)}, f32[32,64,64]{2,1,0:T(8,128)S(1)}, u32[]{:S(2)}) copy-start(f32[32,64,64]{2,1,0:T(8,128)S(1)} %reshape.370) | copy-start | bytes 1572868
  17.5 9.4 %copy-start.5 = (f32[3,32,85]{2,1,0:T(8,128)S(1)}, f32[3,32,85]{2,1,0:T(8,128)}, u32[]{:S(2)}) copy-start(f32[3,32,85]{2,1,0:T(8,128)} %param.12) | copy-start | bytes 97924
  17.5 9.5 %copy-start.4 = (f32[32,32,84]{2,1,0:T(8,128)S(1)}, f32[32,32,84]{2,1,0:T(8,128)}, u32[]{:S(2)}) copy-start(f32[32,32,84]{2,1,0:T(8,128)} %param.11) | copy-start | bytes 1032196
  21.3 117.2 %collective-permute-start.3 = (f32[608,11]{1,0:T(8,128)}, f32[608,11]{1,0:T(8,128)}, u32[]{:S(2)}, u32[]{:S(2)}) collective-permute-start(f32[608,11]{1,0:T(8,128)} %get-tuple-element.124), channel_id=1, source_target_pairs={{1,0},{2,1},{3,2},{4,3},{5,4},{6,5},{7,6},{8,7},{9,8},{10,9},{11,1... | collective-permute-start | bytes 80264 | tf_op jit(solution)/shard_map/ppermute | solution.py:29
  22.6 115.9 %collective-permute-start.2 = (f32[608,11]{1,0:T(8,128)}, f32[608,11]{1,0:T(8,128)}, u32[]{:S(2)}, u32[]{:S(2)}) collective-permute-start(f32[608,11]{1,0:T(8,128)} %get-tuple-element.123), channel_id=1, source_target_pairs={{0,1},{1,2},{2,3},{3,4},{4,5},{5,6},{6,7},{7,8},{8,9},{9,10},{10,1... | collective-permute-start | bytes 80264 | tf_op jit(solution)/shard_map/ppermute | solution.py:27
  30.0 3.8 %copy-start.2 = (f32[32,32,64]{1,0,2:T(8,128)}, f32[32,32,64]{1,0,2:T(8,128)S(1)}, u32[]{:S(2)}) copy-start(f32[32,32,64]{1,0,2:T(8,128)S(1)} %copy.172) | copy-start | bytes 786436
  31.1 4.3 %copy-start.15 = (f32[3,4096]{1,0:T(4,128)S(1)}, f32[3,4096]{1,0:T(4,128)}, u32[]{:S(2)}) copy-start(f32[3,4096]{1,0:T(4,128)} %param.8) | copy-start | bytes 147460
  31.1 4.6 %copy-start.16 = (s32[84,20]{0,1:T(8,128)S(1)}, s32[84,20]{0,1:T(8,128)}, u32[]{:S(2)}) copy-start(s32[84,20]{0,1:T(8,128)} %param.14) | copy-start | bytes 20164
  31.1 5.3 %copy-start.47 = (s32[1,128]{1,0:T(1,128)S(1)}, s32[1,128]{1,0:T(1,128)}, u32[]{:S(2)}) copy-start(s32[1,128]{1,0:T(1,128)} %param.15) | copy-start | bytes 1540
  32.1 126.5 %collective-permute-start.5 = (f32[608,11]{0,1:T(8,128)}, f32[608,11]{0,1:T(8,128)}, u32[]{:S(2)}, u32[]{:S(2)}) collective-permute-start(f32[608,11]{0,1:T(8,128)} %get-tuple-element.141), channel_id=1, source_target_pairs={{1,0},{2,1},{3,2},{4,3},{5,4},{6,5},{7,6},{8,7},{9,8},{10,9},{11,1... | collective-permute-start | bytes 80264 | tf_op jit(solution)/shard_map/ppermute | solution.py:29
  33.8 53.8 %copy-start.6 = (f32[32,32,16]{1,0,2:T(8,128)}, f32[32,32,16]{1,0,2:T(8,128)S(1)}, u32[]{:S(2)}) copy-start(f32[32,32,16]{1,0,2:T(8,128)S(1)} %copy.173) | copy-start | bytes 196612
  35.7 52.8 %copy-start.43 = (s32[64,5]{0,1:T(8,128)S(1)}, s32[64,5]{0,1:T(8,128)}, u32[]{:S(2)}) copy-start(s32[64,5]{0,1:T(8,128)} %param.13) | copy-start | bytes 3844
  37.0 56.5 %copy-start.38 = (pred[128]{0:T(512)(128)(4,1)}, pred[128]{0:T(512)(128)(4,1)S(1)}, u32[]{:S(2)}) copy-start(pred[128]{0:T(512)(128)(4,1)S(1)} %get-tuple-element.152) | copy-start | bytes 388
  91.6 14.8 %copy-start.9 = (f32[19,4096]{1,0:T(8,128)S(1)}, f32[19,4096]{1,0:T(8,128)}, u32[]{:S(2)}) copy-start(f32[19,4096]{1,0:T(8,128)} %copy-done.8) | copy-start | bytes 933892
  92.4 14.8 %copy-start.37 = (s32[1024]{0:T(1024)}, s32[1024]{0:T(1024)S(1)}, u32[]{:S(2)}) copy-start(s32[1024]{0:T(1024)S(1)} %pad_clamp_fusion.1) | copy-start | bytes 12292
  103.9 54.6 %collective-permute-start.4 = (f32[608,11]{0,1:T(8,128)}, f32[608,11]{0,1:T(8,128)S(1)}, u32[]{:S(2)}, u32[]{:S(2)}) collective-permute-start(f32[608,11]{0,1:T(8,128)} %get-tuple-element.140), channel_id=1, source_target_pairs={{0,1},{1,2},{2,3},{3,4},{4,5},{5,6},{6,7},{7,8},{8,9},{9,10},{10,1... | collective-permute-start | bytes 80264 | tf_op jit(solution)/shard_map/ppermute | solution.py:27
  158.5 3.0 %copy-start.30 = (pred[20,16]{1,0:T(8,128)(4,1)S(1)}, pred[20,16]{1,0:T(8,128)(4,1)}, u32[]{:S(2)}) copy-start(pred[20,16]{1,0:T(8,128)(4,1)} %get-tuple-element.61) | copy-start | bytes 964
  163.6 2.0 copy-start.17
  163.6 2.0 copy-start.33
  163.6 2.0 copy-start.34
  163.7 2.0 copy-start.35
  163.7 2.0 copy-start.36
  165.6 9.5 %copy-start.10 = (f32[32,20,64]{0,2,1:T(8,128)S(1)}, f32[32,20,64]{0,2,1:T(8,128)}, u32[]{:S(2)}) copy-start(f32[32,20,64]{0,2,1:T(8,128)} %copy.132) | copy-start | bytes 491524
  165.6 9.5 %copy-start.11 = (f32[32,20,64]{0,2,1:T(8,128)S(1)}, f32[32,20,64]{0,2,1:T(8,128)}, u32[]{:S(2)}) copy-start(f32[32,20,64]{0,2,1:T(8,128)} %copy.130) | copy-start | bytes 491524
  165.6 9.5 %copy-start.12 = (f32[32,20,64]{0,2,1:T(8,128)S(1)}, f32[32,20,64]{0,2,1:T(8,128)}, u32[]{:S(2)}) copy-start(f32[32,20,64]{0,2,1:T(8,128)} %copy.128) | copy-start | bytes 491524
  165.7 9.5 %copy-start.21 = (f32[32,64]{0,1:T(8,128)S(1)}, f32[32,64]{0,1:T(8,128)}, u32[]{:S(2)}) copy-start(f32[32,64]{0,1:T(8,128)} %copy.131) | copy-start | bytes 24580
  165.7 9.5 %copy-start.22 = (f32[32,64]{0,1:T(8,128)S(1)}, f32[32,64]{0,1:T(8,128)}, u32[]{:S(2)}) copy-start(f32[32,64]{0,1:T(8,128)} %copy.129) | copy-start | bytes 24580
  165.7 9.5 %copy-start.23 = (f32[32,64]{0,1:T(8,128)S(1)}, f32[32,64]{0,1:T(8,128)}, u32[]{:S(2)}) copy-start(f32[32,64]{0,1:T(8,128)} %copy.125) | copy-start | bytes 24580
  165.7 9.5 %copy-start.32 = (f32[20,64]{1,0:T(8,128)S(1)}, f32[20,64]{1,0:T(8,128)}, u32[]{:S(2)}) copy-start(f32[20,64]{1,0:T(8,128)} %get-tuple-element.145) | copy-start | bytes 15364
  212.8 3.9 %copy-start.39 = (pred[128]{0:T(512)(128)(4,1)S(1)}, pred[128]{0:T(512)(128)(4,1)}, u32[]{:S(2)}) copy-start(pred[128]{0:T(512)(128)(4,1)} %copy-done.38) | copy-start | bytes 388
  215.7 1.8 copy-start.18
  215.7 1.8 copy-start.19
  215.7 1.8 copy-start.20
  215.7 1.8 copy-start.31
  217.5 2.2 copy-start.27
  217.5 2.2 copy-start.28
  217.5 2.2 copy-start.29
  217.5 2.2 copy-start.44
  217.6 2.2 copy-start.45
  217.6 2.2 copy-start.46
  217.6 2.2 copy-start.48
  217.6 3.2 %copy-start.7 = (f32[32,32,16]{1,0,2:T(8,128)S(1)}, f32[32,32,16]{1,0,2:T(8,128)}, u32[]{:S(2)}) copy-start(f32[32,32,16]{1,0,2:T(8,128)} %copy-done.6) | copy-start | bytes 196612
  220.5 2.6 %copy-start.1 = (f32[32,64,64]{2,1,0:T(8,128)S(1)}, f32[32,64,64]{2,1,0:T(8,128)}, u32[]{:S(2)}) copy-start(f32[32,64,64]{2,1,0:T(8,128)} %copy-done) | copy-start | bytes 1572868
  220.5 2.6 %copy-start.13 = (f32[64,16,64]{2,1,0:T(8,128)S(1)}, f32[64,16,64]{2,1,0:T(8,128)}, u32[]{:S(2)}) copy-start(f32[64,16,64]{2,1,0:T(8,128)} %fusion.144) | copy-start | bytes 786436
  (8 other events, 11.1 us)
Sparse Core Ops, SparseCore 0:
  35.5 79.6 all-gather.1
where the time goes:
time: 236 us; the launch traced here: 233 us
  matrix products  82.3 us (35%)
  local copies, waits for them, and re-layouts  59.8 us (25%)
  blocking collectives  50.5 us (21%)
  between operations  14.5 us (6%)
  starting transfers between devices  14.2 us (6%)
  other arithmetic  11.2 us (5%)
    all_gather x1, blocking collectives, body(): lax.all_gather(stacked_prox, 'leaf', axis=2, tiled=True)  50.5 us
    dot_general x4, matrix products, one_block(): return jnp.einsum('absn,bksn->akn', kernel, coeff_blk, precision=highest)  43.8 us
    dot_general x5, matrix products, near_local(): jnp.einsum('nij,knj->kni', kernel, window[:vectors], precision=highest)  30.2 us
    gather x4, local copies, waits for them, and re-layouts, one_block(): coeff_blk = jnp.take(lookup, clipped_blk, axis=2)  11.2 us
    gather x7, local copies, waits for them, and re-layouts, one_block(): prox_blk = jnp.take(source_prox, clipped_blk, axis=2)  10.4 us
    ppermute x3, starting transfers between devices, with_halo_2(): lax.ppermute(tail, axis, [(i, (i + 1) % count) for i in range(ends)])  10.4 us
    sub x11, local copies, waits for them, and re-layouts, kernel_sq(): left_pts[0] - right_pts[0]  5.53 us
    slice x1, local copies, waits for them, and re-layouts, body(): gathered_coeffs[:, :, :, begin_at:begin_at + extent]  4.78 us
  transfers between devices with their start and end apart: 7, of which 0 were waited for; matrix products, arithmetic and copies ran while one was open for 57% of the time, Pallas kernels for 0%

commit v1 on v0

v1 whole, which is shorter than its diff:
```python
import functools
import math

import jax
import jax.numpy as jnp
from jax import lax
from jax.experimental import pallas as pl
from jax.experimental.pallas import tpu as pltpu
from jax.sharding import PartitionSpec as P

F32, BF16 = jnp.float32, jnp.bfloat16
MESH = pl.DeviceIdType.MESH
BIG = 16384.0
SCALE = math.sqrt(10.0 * math.log2(math.e))
LANES = 128
KN = 64
KC = 80


def nt(a, b):
    return lax.dot_general(a, b, (((1,), (1,)), ((), ())), preferred_element_type=F32)


def nn(a, b):
    return lax.dot_general(a, b, (((1,), (0,)), ((), ())), preferred_element_type=F32)


def iota(shape, dim):
    return lax.broadcasted_iota(jnp.int32, shape, dim)


def halves(x):
    hi = x.astype(BF16)
    return hi, (x - hi.astype(F32)).astype(BF16)


def stacked(x):
    hi = x.astype(BF16).astype(F32)
    return jnp.concatenate([hi, x - hi], axis=0).astype(BF16)


def folded(x):
    n = x.shape[0] // 2
    return x[:n] + x[n:]


def thirds(x):
    h = x.astype(BF16).astype(F32)
    m = (x - h).astype(BF16).astype(F32)
    return h, m, x - h - m


def source_rows(x):
    r = iota(x.shape, 0)
    x = jnp.where(r < 3, x, 0.0)
    n2 = jnp.sum(x * x, axis=0, keepdims=True)
    return jnp.where(r < 3, x, jnp.where(r == 3, n2, jnp.where(r == 4, 1.0, 0.0)))


def target_rows(x):
    r = iota(x.shape, 0)
    x = jnp.where(r < 3, x, 0.0)
    n2 = jnp.sum(x * x, axis=0, keepdims=True)
    return jnp.where(r < 3, 2.0 * x, jnp.where(r == 3, -1.0, jnp.where(r == 4, -n2, 0.0)))


def source_stack(rows):
    h, m, l = thirds(rows)
    return [h, m, l, h, m, h]


def target_stack(rows):
    h, m, l = thirds(rows)
    return [h, h, h, m, m, l]


def gauss(e):
    g = jnp.exp2(e)
    return halves(g)


def kernel(
    n_dev,
    pts_ref, rhs_ref, basis_ref, tr_ref, px_ref, nl_ref, cl_ref, rl_ref,
    out_ref,
    p8, pa, tb, tbh, tbl, eye_ref, bmask,
    ytn, chn, xn, ytc, chc, xc, clb, nlb, rb,
    gc, fc,
    sn, rn, sl, rlr, s1, r1, sq, rq, rg,
    sem_s, sem_r, gs_sem, gr_sem,
):
    me = lax.axis_index("leaf")
    quads = n_dev // 4
    quad, seat = me // 4, me % 4
    left, right = (me + n_dev - 1) % n_dev, (me + 1) % n_dev
    left2, right2 = (me + n_dev - 2) % n_dev, (me + 2) % n_dev
    peers = [quad * 4 + (seat + o) % 4 for o in range(1, 4)]

    def dst(o):
        return ((quad + o) % quads) * 4 + seat

    barrier = pltpu.get_barrier_semaphore()
    for d in [left, right, left2, right2, *peers]:
        pl.semaphore_signal(barrier, inc=1, device_id=(d,), device_id_type=MESH)

    def greet(o, c):
        pl.semaphore_signal(barrier, inc=1, device_id=(dst(o),), device_id_type=MESH)
        return c

    lax.fori_loop(1, quads, greet, 0)

    p8[...] = jnp.zeros_like(p8)
    p8[0:3, :] = (pts_ref[...] - 0.5) * SCALE
    for i, u in ((0, 0), (1, 31)):
        sn[i, 0:16, :] = rhs_ref[:, u * LANES : (u + 1) * LANES]
        sn[i, 16:24, :] = source_rows(p8[:, u * LANES : (u + 1) * LANES])

    pl.semaphore_wait(barrier, 7 + quads - 1)

    def remote(src, dst_ref, i, d):
        return pltpu.make_async_remote_copy(
            src_ref=src, dst_ref=dst_ref, send_sem=sem_s.at[i], recv_sem=sem_r.at[i],
            device_id=(d,), device_id_type=MESH,
        )

    near_copies = [
        remote(sn.at[0], rn.at[1], 0, left),
        remote(sn.at[1], rn.at[0], 1, right),
    ]
    for c in near_copies:
        c.start()

    eye_ref[...] = jnp.where(iota((LANES, LANES), 0) == iota((LANES, LANES), 1), 1.0, 0.0).astype(BF16)
    bmask[...] = jnp.where(iota((LANES, 256), 0) // 32 == iota((LANES, 256), 1) // 64, 1.0, 0.0).astype(BF16)

    lane_n, row_n = iota((LANES, 84), 1), iota((LANES, 84), 0)
    tmask = (lane_n < 4) | (((lane_n >> 2) + 3) % 4 == (row_n >> 5))
    eye84 = jnp.where(iota((84, 84), 0) == iota((84, 84), 1), 1.0, 0.0).astype(BF16)

    def turn(a, c):
        w = tr_ref[a]
        w = jnp.where(tmask, jnp.concatenate([w, w, w, w], axis=0), 0.0)
        hi, lo = halves(w)
        tb[pl.ds(a, 84, stride=32), :] = nt(eye84, hi) + nt(eye84, lo)
        return c

    lax.fori_loop(0, 32, turn, 0)

    def part(i, c):
        hi, lo = halves(tb[pl.ds(i * LANES, LANES), :])
        tbh[i] = hi
        tbl[i] = lo
        return c

    lax.fori_loop(0, 21, part, 0)

    pick = jnp.where(
        ((iota((24, 85), 1) >= 1) & ((iota((24, 85), 1) - 1) >> 2 == iota((24, 85), 0)))
        | ((iota((24, 85), 1) == 0) & (iota((24, 85), 0) == 21)), 1.0, 0.0).astype(BF16)
    lane_p, row_p = iota((LANES, 85), 1), iota((LANES, 85), 0)
    pmask = (lane_p == 0) | ((lane_p + 3) % 4 == (row_p >> 5))
    pa[...] = jnp.zeros_like(pa)
    for ax in range(3):
        w = (px_ref[ax] - 0.5) * SCALE
        w = jnp.where(pmask, jnp.concatenate([w, w, w, w], axis=0), 0.0)
        h, m, l = thirds(w)
        pa[pl.ds(ax, 24, stride=8), :] = (
            nt(pick, h.astype(BF16)) + nt(pick, m.astype(BF16)) + nt(pick, l.astype(BF16))
        )

    def basis_parts(q):
        hi, lo = halves(basis_ref[:, pl.ds(q * 256, 256)])
        mask = bmask[...]
        return (
            jnp.concatenate([hi, hi, hi, hi], axis=0) * mask,
            jnp.concatenate([lo, lo, lo, lo], axis=0) * mask,
        )

    def place(level, q):
        return {1: 28, 2: 20, 3: 0}[level] + 2 + q, {1: 0, 2: 1, 3: 5}[level] + q

    coef3 = gc

    def leaf_coef(q, c):
        bh, bl = basis_parts(q)
        v = stacked(rhs_ref[:, pl.ds(q * 256, 256)])
        coef3[5 + q] = folded(nt(v, bh) + nt(v, bl))
        return c

    lax.fori_loop(0, 16, leaf_coef, 0)

    for r in range(4):
        acc = jnp.zeros((32, LANES), F32)
        for i in range(4):
            b = stacked(coef3[5 + 4 * r + i])
            acc += nn(b, tbh[5 + 4 * r + i]) + nn(b, tbl[5 + 4 * r + i])
        coef3[1 + r] = folded(acc)
    acc = jnp.zeros((32, LANES), F32)
    for i in range(4):
        b = stacked(coef3[1 + i])
        acc += nn(b, tbh[1 + i]) + nn(b, tbl[1 + i])
    coef3[0] = folded(acc)
    b = stacked(coef3[0])
    coef0 = folded(nn(b, tbh[0]) + nn(b, tbl[0]))

    sq[0:16, :] = coef0
    sq[16:24, :] = source_rows(pa[21 * 8 : 22 * 8, :])
    for i, (to_left, to_right) in enumerate(((5, 19), (6, 20), (1, 3), (2, 4), (0, 0))):
        for side, u in ((0, to_left), (1, to_right)):
            sl[side, i, 0:16, :] = coef3[u]
            sl[side, i, 16:24, :] = source_rows(pa[u * 8 : u * 8 + 8, :])
    s1[0:16, :] = coef3[0]
    s1[16:24, :] = source_rows(pa[0:8, :])
    rq[seat] = sq[...]
    quad_copies = [
        pltpu.make_async_remote_copy(
            src_ref=sq, dst_ref=rq.at[seat], send_sem=sem_s.at[6 + o], recv_sem=sem_r.at[6 + seat],
            device_id=(peers[o],), device_id_type=MESH,
        )
        for o in range(3)
    ]
    for c in quad_copies:
        c.start()
    level_copies = [
        remote(sl.at[0], rlr.at[1], 2, left),
        remote(sl.at[1], rlr.at[0], 3, right),
        remote(s1, r1.at[1], 4, left2),
        remote(s1, r1.at[0], 5, right2),
    ]
    for c in level_copies:
        c.start()

    clb[...] = jnp.full_like(clb, -BIG)
    clb[0:20, 0:84] = jnp.where(cl_ref[...] >= 0, 0.0, -BIG)
    nlb[...] = jnp.full_like(nlb, -BIG)
    nlb[0:5, 0:64] = jnp.where(nl_ref[...] >= 0, 0.0, -BIG)
    nb = nlb[...]
    nlb[...] = jnp.where(iota((8, LANES), 1) % 2 == 1, pltpu.roll(nb, 1, axis=0), nb)
    sel4 = jnp.where(iota((LANES, LANES), 0) == iota((LANES, LANES), 1) >> 5, 1.0, 0.0).astype(BF16)
    sel2 = jnp.where(iota((LANES, LANES), 0) == iota((LANES, LANES), 1) >> 6, 1.0, 0.0).astype(BF16)
    selm = jnp.where(iota((LANES, LANES), 0) % 4 == iota((LANES, LANES), 1) >> 5, 1.0, 0.0).astype(BF16)
    rlist = jnp.where(rl_ref[...] >= 0, 0.0, -BIG) + jnp.zeros((32, LANES), F32)
    rlist = jnp.where(iota((32, LANES), 1) >> 2 == iota((32, LANES), 0), rlist, 0.0)
    rb[...] = nn(rlist.astype(BF16), selm)

    def near_source(slab, values, rows):
        cls = (2 * slab + (iota((8, LANES), 1) >> 6)) % 8
        hot = jnp.where(iota((8, LANES), 0) == cls, 1.0, 0.0)
        f = jnp.concatenate([*source_stack(rows), hot, jnp.zeros((8, LANES), F32)], axis=0)
        ytn[pl.ds(pl.multiple_of(slab * LANES, LANES), LANES), :] = nt(eye_ref[...], f.astype(BF16)).astype(BF16)
        chn[slab] = stacked(values)

    def near_prep(u, c):
        at = pl.ds(pl.multiple_of(u * LANES, LANES), LANES)
        x = p8[:, at]
        near_source(u + 1, rhs_ref[:, at], source_rows(x))
        bias = pltpu.roll(pltpu.roll(nlb[...], (LANES - 2 * u) % LANES, axis=1), (2 * u) % 8, axis=0)
        bias = nn(bias.astype(BF16), sel2)
        xn[u] = jnp.concatenate(
            [*target_stack(target_rows(x)), bias, jnp.zeros((8, LANES), F32)], axis=0).astype(BF16)
        return c

    lax.fori_loop(0, 32, near_prep, 0)
    for c in near_copies:
        c.wait()
    near_source(0, rn[0, 0:16, :], rn[0, 16:24, :])
    near_source(33, rn[1, 0:16, :], rn[1, 16:24, :])

    def near_unit(u, c):
        acc = jnp.zeros((32, LANES), F32)
        at = pl.multiple_of(u * LANES, LANES)
        gh, gl = gauss(nn(ytn[pl.ds(at, 3 * LANES), :], xn[u]))
        v = jnp.concatenate([chn[u], chn[u + 1], chn[u + 2]], axis=1)
        acc = nn(v, gh) + nn(v, gl)
        out_ref[:, pl.ds(at, LANES)] = folded(acc)
        return c

    lax.fori_loop(0, 16, near_unit, 0)

    for o in range(3):
        quad_copies[o].wait_send()
    for o in range(1, 4):
        frm = (seat + o) % 4
        pltpu.make_async_remote_copy(
            src_ref=sq, dst_ref=rq.at[frm], send_sem=sem_s.at[6], recv_sem=sem_r.at[6 + frm],
            device_id=(left,), device_id_type=MESH,
        ).wait_recv()
    group = iota((24, LANES), 1) >> 5
    merged = jnp.where(group == 0, rq[0], jnp.where(group == 1, rq[1], jnp.where(group == 2, rq[2], rq[3])))
    sq2 = sn
    sq2[0] = merged
    rg[quad] = merged

    def root_copy(o, slot):
        return pltpu.make_async_remote_copy(
            src_ref=sq2.at[0], dst_ref=rg.at[slot], send_sem=gs_sem.at[o], recv_sem=gr_sem.at[slot],
            device_id=(dst(o),), device_id_type=MESH,
        )

    def root_send(o, c):
        root_copy(o, quad).start()
        return c

    lax.fori_loop(1, quads, root_send, 0)

    lax.fori_loop(16, 32, near_unit, 0)

    def level_source(slab, q_class, values, rows):
        cls = (4 * q_class + (iota((32, LANES), 1) >> 5)) % 32
        hot = jnp.where(iota((32, LANES), 0) == cls, 1.0, 0.0)
        f = jnp.concatenate([*source_stack(rows), hot], axis=0)
        at = slab * LANES if isinstance(slab, int) else pl.multiple_of(slab * LANES, LANES)
        ytc[pl.ds(at, LANES), :] = nt(eye_ref[...], f.astype(BF16)).astype(BF16)
        chc[slab] = stacked(values)

    def level_prep(u, c):
        q = jnp.where(u >= 5, u - 5, jnp.where(u >= 1, u - 1, 0))
        slab = jnp.where(u >= 5, 0, jnp.where(u >= 1, 20, 28)) + 2 + q
        x = pa[pl.ds(pl.multiple_of(u * 8, 8), 8), :]
        level_source(slab, q + 2, coef3[u], source_rows(x))
        bias = pltpu.roll(pltpu.roll(clb[...], (LANES - 4 * u) % LANES, axis=1), (4 * q) % 32, axis=0)
        bias = nn(bias.astype(BF16), sel4)
        xc[u] = jnp.concatenate([*target_stack(target_rows(x)), bias], axis=0).astype(BF16)
        return c

    lax.fori_loop(0, 21, level_prep, 0)
    for c in level_copies:
        c.wait()
    for i in range(2):
        for first, k, n in ((0, 0, 16), (20, 2, 4)):
            level_source(first + i, i, rlr[0, k + i, 0:16, :], rlr[0, k + i, 16:24, :])
            level_source(first + 2 + n + i, 2 + n + i, rlr[1, k + i, 0:16, :], rlr[1, k + i, 16:24, :])
    for i, blk in ((0, r1[0]), (1, rlr[0, 4]), (3, rlr[1, 4]), (4, r1[1])):
        level_source(28 + i, i, blk[0:16], blk[16:24])

    def couple_unit(u, c):
        q = jnp.where(u >= 5, u - 5, jnp.where(u >= 1, u - 1, 0))
        slab = jnp.where(u >= 5, 0, jnp.where(u >= 1, 20, 28)) + q
        at = pl.multiple_of(slab * LANES, LANES)
        gh, gl = gauss(nn(ytc[pl.ds(at, 5 * LANES), :], xc[u]))
        v = jnp.concatenate([chc[slab + i] for i in range(5)], axis=1)
        fc[u] = folded(nn(v, gh) + nn(v, gl))
        return c

    lax.fori_loop(0, 21, couple_unit, 0)

    froot = jnp.concatenate(target_stack(target_rows(pa[21 * 8 : 22 * 8, :])), axis=0)
    troot = nt(eye_ref[0:32, :], froot.astype(BF16)).astype(BF16)

    def root_wait(o, c):
        root_copy(o, (quad + quads - o) % quads).wait_recv()
        return c

    lax.fori_loop(1, quads, root_wait, 0)

    def root_unit(u, acc):
        f = jnp.concatenate(source_stack(rg[u, 16:24, :]), axis=0)
        gh, gl = gauss(nn(troot, f.astype(BF16)) + rb[pl.ds(u, 1), :])
        return acc + nt(stacked(rg[u, 0:16, :]), jnp.concatenate([gh, gl], axis=0))

    acc = lax.fori_loop(0, quads, root_unit, jnp.zeros((32, 64), F32))
    acc = folded(acc)
    f0 = jnp.concatenate([acc, jnp.zeros((16, 64), F32)], axis=1)

    def down(f, u):
        b = stacked(f)
        fc[u] += folded(nt(b, tbh[u]) + nt(b, tbl[u]))

    down(f0, 0)
    f1 = fc[0]
    for q in range(4):
        down(f1, 1 + q)

    def far(q, c):
        down(fc[1 + q // 4], 5 + q)
        bh, bl = basis_parts(q)
        b = stacked(fc[5 + q])
        out_ref[:, pl.ds(pl.multiple_of(q * 256, 256), 256)] += folded(nn(b, bh) + nn(b, bl))
        return c

    lax.fori_loop(0, 16, far, 0)

    for c in near_copies[:0]:
        c.wait()

    def root_done(o, c):
        root_copy(o, quad).wait_send()
        return c

    lax.fori_loop(1, quads, root_done, 0)


def body(n_dev, points, rhs, leaf_basis, transfer, proxies, near_list, couple_list, root_list):
    rlist = root_list
    if n_dev < LANES:
        rlist = jnp.pad(rlist, ((0, 0), (0, LANES - n_dev)))
    quads = n_dev // 4
    scratch = [
        pltpu.VMEM((8, 4096), F32),
        pltpu.VMEM((192, LANES), F32),
        pltpu.VMEM((84 * 32, LANES), F32),
        pltpu.VMEM((21, LANES, LANES), BF16),
        pltpu.VMEM((21, LANES, LANES), BF16),
        pltpu.VMEM((LANES, LANES), BF16),
        pltpu.VMEM((LANES, 256), BF16),
        pltpu.VMEM((34 * LANES, KN), BF16),
        pltpu.VMEM((34, 32, LANES), BF16),
        pltpu.VMEM((32, KN, LANES), BF16),
        pltpu.VMEM((33 * LANES, KC), BF16),
        pltpu.VMEM((33, 32, LANES), BF16),
        pltpu.VMEM((21, KC, LANES), BF16),
        pltpu.VMEM((32, LANES), F32),
        pltpu.VMEM((8, LANES), F32),
        pltpu.VMEM((32, LANES), F32),
        pltpu.VMEM((21, 16, LANES), F32),
        pltpu.VMEM((21, 16, LANES), F32),
        pltpu.VMEM((2, 24, LANES), F32),
        pltpu.VMEM((2, 24, LANES), F32),
        pltpu.VMEM((2, 5, 24, LANES), F32),
        pltpu.VMEM((2, 5, 24, LANES), F32),
        pltpu.VMEM((24, LANES), F32),
        pltpu.VMEM((2, 24, LANES), F32),
        pltpu.VMEM((24, LANES), F32),
        pltpu.VMEM((4, 24, LANES), F32),
        pltpu.VMEM((quads, 24, LANES), F32),
        pltpu.SemaphoreType.DMA((10,)),
        pltpu.SemaphoreType.DMA((10,)),
        pltpu.SemaphoreType.DMA((quads,)),
        pltpu.SemaphoreType.DMA((quads,)),
    ]
    vmem = pl.BlockSpec(memory_space=pltpu.VMEM)
    return pl.pallas_call(
        functools.partial(kernel, n_dev),
        out_shape=jax.ShapeDtypeStruct(rhs.shape, F32),
        in_specs=[vmem] * 8,
        out_specs=vmem,
        scratch_shapes=scratch,
        compiler_params=pltpu.CompilerParams(
            collective_id=0, has_side_effects=True, vmem_limit_bytes=40 * 2**20
        ),
        name="hmatvec",
    )(points, rhs, leaf_basis, transfer, proxies, near_list.T, couple_list.T, rlist)


def solution(mesh):
    n_dev = mesh.shape["leaf"]
    in_specs = (
        P(None, "leaf"), P(None, "leaf"), P(None, "leaf"), P(None, None, "leaf"), P(None, None, "leaf"),
        P("leaf", None), P("leaf", None), P("leaf", None),
    )
    return jax.shard_map(
        functools.partial(body, n_dev), mesh=mesh, in_specs=in_specs, out_specs=P(None, "leaf"), check_vma=False
    )
```

time: 236 us -> 72.5 us (0.31); the launches traced: 233 us -> 71.7 us
  matrix products: 82.3 us -> 0 us
  Pallas kernels: 0 us -> 64.2 us
  local copies, waits for them, and re-layouts: 59.8 us -> 7.42 us
  blocking collectives: 50.5 us -> 0 us
  between operations: 14.5 us -> 0.02 us
  starting transfers between devices: 14.2 us -> 0 us
  other arithmetic: 11.2 us -> 0 us
    dot_general x17 -> x0, matrix products: 82.3 us -> none  [the longest x4 43.8 us: one_block(): return jnp.einsum('absn,bksn->akn', kernel, coeff_blk, precision=highest)]
    pallas_call x0 -> x1, Pallas kernels: none -> 64.2 us  [body(): pl.pallas_call(functools.partial(kernel, n_dev), out_shape=jax.ShapeDtype...]
    all_gather x1 -> x0, blocking collectives: 50.5 us -> none  [body(): lax.all_gather(stacked_prox, 'leaf', axis=2, tiled=True)]
    gather x11 -> x0, local copies, waits for them, and re-layouts: 21.6 us -> none  [the longest x4 11.2 us: one_block(): coeff_blk = jnp.take(lookup, clipped_blk, axis=2)]
    ppermute x6 -> x0, starting transfers between devices: 14.2 us -> none  [the longest x3 10.4 us: with_halo_2(): lax.ppermute(tail, axis, [(i, (i + 1) % count) for i in range(ends)])]
    sub x21 -> x0, local copies, waits for them, and re-layouts: 13.1 us -> none  [the longest x11 5.53 us: kernel_sq(): left_pts[0] - right_pts[0]]
    slice x20 -> x0, local copies, waits for them, and re-layouts: 11.3 us -> none  [the longest x1 4.78 us: body(): gathered_coeffs[:, :, :, begin_at:begin_at + extent]]
    reshape x13 -> x0, local copies, waits for them, and re-layouts: 6.78 us -> none  [the longest x1 1.46 us: body(): basis_grid = leaf_basis.reshape(rank_dim, leaves, LEAF)]
  transfers between devices with their start and end apart: 7 -> 0, of which waited for: 0 -> 0; matrix products, arithmetic and copies ran while one was open for 57% -> 0% of each run, Pallas kernels for 0% -> 0%
where the time goes in v1:
time: 72.5 us; the launch traced here: 71.7 us
  Pallas kernels  64.2 us (89%)
  local copies, waits for them, and re-layouts  7.42 us (10%)
    pallas_call x1, Pallas kernels, body(): pl.pallas_call(functools.partial(kernel, n_dev), out_shape=jax.ShapeDtype...  64.2 us
    unnamed x17, local copies, waits for them, and re-layouts  7.42 us

profile of v1, /device:TPU:0, one launch (start us, length us, event | category | flops | bytes accessed | tf_op | source)
XLA Modules:
  0.0 71.7 jit_solution(5522138270825982086)
XLA Ops:
  0.0 0.0 copy-start.7
  0.0 0.7 copy-done.7
  0.7 0.0 copy-start
  0.7 1.0 %copy-done = f32[32,4096]{1,0:T(8,128)S(1)} copy-done((f32[32,4096]{1,0:T(8,128)S(1)}, f32[32,4096]{1,0:T(8,128)}, u32[]{:S(2)}) %copy-start) | copy-done | bytes 524312
  1.7 0.0 copy-start.1
  1.7 1.0 %copy-done.1 = f32[32,32,84]{2,1,0:T(8,128)S(1)} copy-done((f32[32,32,84]{2,1,0:T(8,128)S(1)}, f32[32,32,84]{2,1,0:T(8,128)}, u32[]{:S(2)}) %copy-start.1) | copy-done | bytes 344088
  2.7 0.0 copy-start.2
  2.7 0.9 %copy-done.2 = f32[16,4096]{1,0:T(8,128)S(1)} copy-done((f32[16,4096]{1,0:T(8,128)S(1)}, f32[16,4096]{1,0:T(8,128)}, u32[]{:S(2)}) %copy-start.2) | copy-done | bytes 262168
  3.7 0.0 copy-start.3
  3.7 0.8 %copy-done.3 = f32[3,4096]{1,0:T(4,128)S(1)} copy-done((f32[3,4096]{1,0:T(4,128)S(1)}, f32[3,4096]{1,0:T(4,128)}, u32[]{:S(2)}) %copy-start.3) | copy-done | bytes 49176
  4.5 0.0 copy-start.4
  4.5 0.8 %copy-done.4 = f32[3,32,85]{2,1,0:T(8,128)S(1)} copy-done((f32[3,32,85]{2,1,0:T(8,128)S(1)}, f32[3,32,85]{2,1,0:T(8,128)}, u32[]{:S(2)}) %copy-start.4) | copy-done | bytes 32664
  5.3 0.0 copy-start.5
  5.3 0.7 copy-done.5
  6.0 0.0 copy-start.6
  6.0 0.7 copy-done.6
  6.7 64.2 %hmatvec.1 = f32[16,4096]{1,0:T(8,128)S(1)} custom-call(f32[3,4096]{1,0:T(4,128)S(1)} %copy-done.3, f32[16,4096]{1,0:T(8,128)S(1)} %copy-done.2, f32[32,4096]{1,0:T(8,128)S(1)} %copy-done, f32[32,32,84]{2,1,0:T(8,128)S(1)} %copy-done.1, f32[3,32,85]{2,1,0:T(8,128)S(1)} %copy-done.4, s32[5,64]{1,0:T(8,128)S(1)} %bitcast.3, s32[20,84]{1,0:T(8,128)S(1)} %bitcast.2, ...), custom_call_target="tpu_custom_call" | custom-call | tf_op jit(solution)/shard_map/hmatvec/pallas_call | solution.py:432
  71.0 0.7 copy.10
Async XLA Ops:
  0.0 0.7 copy-start.7
  0.7 1.0 %copy-start = (f32[32,4096]{1,0:T(8,128)S(1)}, f32[32,4096]{1,0:T(8,128)}, u32[]{:S(2)}) copy-start(f32[32,4096]{1,0:T(8,128)} %basis_ref.1) | copy-start | bytes 1572868
  1.7 1.0 %copy-start.1 = (f32[32,32,84]{2,1,0:T(8,128)S(1)}, f32[32,32,84]{2,1,0:T(8,128)}, u32[]{:S(2)}) copy-start(f32[32,32,84]{2,1,0:T(8,128)} %tr_ref.1) | copy-start | bytes 1032196
  2.7 0.9 %copy-start.2 = (f32[16,4096]{1,0:T(8,128)S(1)}, f32[16,4096]{1,0:T(8,128)}, u32[]{:S(2)}) copy-start(f32[16,4096]{1,0:T(8,128)} %rhs_ref.1) | copy-start | bytes 786436
  3.7 0.8 %copy-start.3 = (f32[3,4096]{1,0:T(4,128)S(1)}, f32[3,4096]{1,0:T(4,128)}, u32[]{:S(2)}) copy-start(f32[3,4096]{1,0:T(4,128)} %pts_ref.1) | copy-start | bytes 147460
  4.5 0.8 %copy-start.4 = (f32[3,32,85]{2,1,0:T(8,128)S(1)}, f32[3,32,85]{2,1,0:T(8,128)}, u32[]{:S(2)}) copy-start(f32[3,32,85]{2,1,0:T(8,128)} %px_ref.1) | copy-start | bytes 97924
  5.3 0.7 copy-start.5
  6.0 0.7 copy-start.6

commit v2 on v1

--- a/solution.py
+++ b/solution.py
@@ -81,14 +81,25 @@
 
 def kernel(
     n_dev,
-    pts_ref, rhs_ref, basis_ref, tr_ref, px_ref, nl_ref, cl_ref, rl_ref,
+    pts_hbm, rhs_hbm, basis_hbm, tr_hbm, px_hbm, nl_hbm, cl_hbm, rl_hbm,
     out_ref,
-    p8, pa, tb, tbh, tbl, eye_ref, bmask,
-    ytn, chn, xn, ytc, chc, xc, clb, nlb, rb,
-    gc, fc,
+    pts_ref, rhs_ref, basis_ref, tr_ref, px_ref, nl_ref, cl_ref, rl_ref, in_sem,
+    nr, p8, pa, tb, tbh, tbl, eye_ref, bmask,
+    ytn, chn, xn, ytc, chc, xc, xc1, clb, nlb, rb,
+    gc, fc, fd,
     sn, rn, sl, rlr, s1, r1, sq, rq, rg,
     sem_s, sem_r, gs_sem, gr_sem,
 ):
+    loads = {
+        name: pltpu.make_async_copy(src, dst, in_sem.at[i])
+        for i, (name, src, dst) in enumerate((
+            ("tr", tr_hbm, tr_ref), ("px", px_hbm, px_ref), ("basis", basis_hbm, basis_ref),
+            ("rhs", rhs_hbm, rhs_ref), ("pts", pts_hbm, pts_ref), ("nl", nl_hbm, nl_ref),
+            ("cl", cl_hbm, cl_ref), ("rl", rl_hbm, rl_ref),
+        ))
+    }
+    for c in loads.values():
+        c.start()
     me = lax.axis_index("leaf")
     quads = n_dev // 4
     quad, seat = me // 4, me % 4
@@ -109,30 +120,10 @@
 
     lax.fori_loop(1, quads, greet, 0)
 
-    p8[...] = jnp.zeros_like(p8)
-    p8[0:3, :] = (pts_ref[...] - 0.5) * SCALE
-    for i, u in ((0, 0), (1, 31)):
-        sn[i, 0:16, :] = rhs_ref[:, u * LANES : (u + 1) * LANES]
-        sn[i, 16:24, :] = source_rows(p8[:, u * LANES : (u + 1) * LANES])
-
-    pl.semaphore_wait(barrier, 7 + quads - 1)
-
-    def remote(src, dst_ref, i, d):
-        return pltpu.make_async_remote_copy(
-            src_ref=src, dst_ref=dst_ref, send_sem=sem_s.at[i], recv_sem=sem_r.at[i],
-            device_id=(d,), device_id_type=MESH,
-        )
-
-    near_copies = [
-        remote(sn.at[0], rn.at[1], 0, left),
-        remote(sn.at[1], rn.at[0], 1, right),
-    ]
-    for c in near_copies:
-        c.start()
-
     eye_ref[...] = jnp.where(iota((LANES, LANES), 0) == iota((LANES, LANES), 1), 1.0, 0.0).astype(BF16)
     bmask[...] = jnp.where(iota((LANES, 256), 0) // 32 == iota((LANES, 256), 1) // 64, 1.0, 0.0).astype(BF16)
 
+    loads["tr"].wait()
     lane_n, row_n = iota((LANES, 84), 1), iota((LANES, 84), 0)
     tmask = (lane_n < 4) | (((lane_n >> 2) + 3) % 4 == (row_n >> 5))
     eye84 = jnp.where(iota((84, 84), 0) == iota((84, 84), 1), 1.0, 0.0).astype(BF16)
@@ -144,7 +135,7 @@
         tb[pl.ds(a, 84, stride=32), :] = nt(eye84, hi) + nt(eye84, lo)
         return c
 
-    lax.fori_loop(0, 32, turn, 0)
+    lax.fori_loop(0, 32, turn, 0, unroll=4)
 
     def part(i, c):
         hi, lo = halves(tb[pl.ds(i * LANES, LANES), :])
@@ -152,8 +143,9 @@
         tbl[i] = lo
         return c
 
-    lax.fori_loop(0, 21, part, 0)
-
+    lax.fori_loop(0, 21, part, 0, unroll=3)
+
+    loads["px"].wait()
     pick = jnp.where(
         ((iota((24, 85), 1) >= 1) & ((iota((24, 85), 1) - 1) >> 2 == iota((24, 85), 0)))
         | ((iota((24, 85), 1) == 0) & (iota((24, 85), 0) == 21)), 1.0, 0.0).astype(BF16)
@@ -176,9 +168,8 @@
             jnp.concatenate([lo, lo, lo, lo], axis=0) * mask,
         )
 
-    def place(level, q):
-        return {1: 28, 2: 20, 3: 0}[level] + 2 + q, {1: 0, 2: 1, 3: 5}[level] + q
-
+    loads["basis"].wait()
+    loads["rhs"].wait()
     coef3 = gc
 
     def leaf_coef(q, c):
@@ -187,7 +178,7 @@
         coef3[5 + q] = folded(nt(v, bh) + nt(v, bl))
         return c
 
-    lax.fori_loop(0, 16, leaf_coef, 0)
+    lax.fori_loop(0, 16, leaf_coef, 0, unroll=4)
 
     for r in range(4):
         acc = jnp.zeros((32, LANES), F32)
@@ -202,6 +193,14 @@
     coef3[0] = folded(acc)
     b = stacked(coef3[0])
     coef0 = folded(nn(b, tbh[0]) + nn(b, tbl[0]))
+
+    pl.semaphore_wait(barrier, 7 + quads - 1)
+
+    def remote(src, dst_ref, i, d):
+        return pltpu.make_async_remote_copy(
+            src_ref=src, dst_ref=dst_ref, send_sem=sem_s.at[i], recv_sem=sem_r.at[i],
+            device_id=(d,), device_id_type=MESH,
+        )
 
     sq[0:16, :] = coef0
     sq[16:24, :] = source_rows(pa[21 * 8 : 22 * 8, :])
@@ -230,14 +229,37 @@
     for c in level_copies:
         c.start()
 
+    loads["pts"].wait()
+    p8[...] = jnp.zeros_like(p8)
+    p8[0:3, :] = (pts_ref[...] - 0.5) * SCALE
+    for i, u in ((0, 0), (1, 31)):
+        sn[i, 0:16, :] = rhs_ref[:, u * LANES : (u + 1) * LANES]
+        sn[i, 16:24, :] = source_rows(p8[:, u * LANES : (u + 1) * LANES])
+
+    near_copies = [
+        remote(sn.at[0], rn.at[1], 0, left),
+        remote(sn.at[1], rn.at[0], 1, right),
+    ]
+    for c in near_copies:
+        c.start()
+
+    for name in ("nl", "cl", "rl"):
+        loads[name].wait()
+
     clb[...] = jnp.full_like(clb, -BIG)
     clb[0:20, 0:84] = jnp.where(cl_ref[...] >= 0, 0.0, -BIG)
     nlb[...] = jnp.full_like(nlb, -BIG)
     nlb[0:5, 0:64] = jnp.where(nl_ref[...] >= 0, 0.0, -BIG)
     nb = nlb[...]
-    nlb[...] = jnp.where(iota((8, LANES), 1) % 2 == 1, pltpu.roll(nb, 1, axis=0), nb)
-    sel4 = jnp.where(iota((LANES, LANES), 0) == iota((LANES, LANES), 1) >> 5, 1.0, 0.0).astype(BF16)
-    sel2 = jnp.where(iota((LANES, LANES), 0) == iota((LANES, LANES), 1) >> 6, 1.0, 0.0).astype(BF16)
+    h = iota((8, LANES), 1) % 4
+    for k in range(1, 4):
+        nb = jnp.where(h == k, pltpu.roll(nlb[...], k, axis=0), nb)
+    nlb[...] = nb
+    cb = clb[...]
+    clb[...] = jnp.where((iota((32, LANES), 1) + 4) % 8 >= 4, pltpu.roll(cb, 4, axis=0), cb)
+    c1b = cb
+    sel8 = jnp.where(iota((LANES, 256), 0) == iota((LANES, 256), 1) >> 5, 1.0, 0.0).astype(BF16)
+    sel4 = jnp.where(iota((LANES, 256), 0) == iota((LANES, 256), 1) >> 6, 1.0, 0.0).astype(BF16)
     selm = jnp.where(iota((LANES, LANES), 0) % 4 == iota((LANES, LANES), 1) >> 5, 1.0, 0.0).astype(BF16)
     rlist = jnp.where(rl_ref[...] >= 0, 0.0, -BIG) + jnp.zeros((32, LANES), F32)
     rlist = jnp.where(iota((32, LANES), 1) >> 2 == iota((32, LANES), 0), rlist, 0.0)
@@ -250,32 +272,30 @@
         ytn[pl.ds(pl.multiple_of(slab * LANES, LANES), LANES), :] = nt(eye_ref[...], f.astype(BF16)).astype(BF16)
         chn[slab] = stacked(values)
 
-    def near_prep(u, c):
-        at = pl.ds(pl.multiple_of(u * LANES, LANES), LANES)
-        x = p8[:, at]
-        near_source(u + 1, rhs_ref[:, at], source_rows(x))
-        bias = pltpu.roll(pltpu.roll(nlb[...], (LANES - 2 * u) % LANES, axis=1), (2 * u) % 8, axis=0)
-        bias = nn(bias.astype(BF16), sel2)
-        xn[u] = jnp.concatenate(
-            [*target_stack(target_rows(x)), bias, jnp.zeros((8, LANES), F32)], axis=0).astype(BF16)
-        return c
-
-    lax.fori_loop(0, 32, near_prep, 0)
+    def near_prep(v, c):
+        for i in range(2):
+            at = pl.ds(pl.multiple_of((2 * v + i) * LANES, LANES), LANES)
+            near_source(2 * v + i + 1, rhs_ref[:, at], source_rows(p8[:, at]))
+        x = p8[:, pl.ds(pl.multiple_of(v * 256, 256), 256)]
+        bias = pltpu.roll(pltpu.roll(nlb[...], (LANES - 4 * v) % LANES, axis=1), (4 * v) % 8, axis=0)
+        bias = nn(bias.astype(BF16), sel4)
+        xn[v] = jnp.concatenate(
+            [*target_stack(target_rows(x)), bias, jnp.zeros((8, 256), F32)], axis=0).astype(BF16)
+        return c
+
+    lax.fori_loop(0, 16, near_prep, 0, unroll=4)
     for c in near_copies:
         c.wait()
     near_source(0, rn[0, 0:16, :], rn[0, 16:24, :])
     near_source(33, rn[1, 0:16, :], rn[1, 16:24, :])
 
-    def near_unit(u, c):
-        acc = jnp.zeros((32, LANES), F32)
-        at = pl.multiple_of(u * LANES, LANES)
-        gh, gl = gauss(nn(ytn[pl.ds(at, 3 * LANES), :], xn[u]))
-        v = jnp.concatenate([chn[u], chn[u + 1], chn[u + 2]], axis=1)
-        acc = nn(v, gh) + nn(v, gl)
-        out_ref[:, pl.ds(at, LANES)] = folded(acc)
-        return c
-
-    lax.fori_loop(0, 16, near_unit, 0)
+    def near_unit(v, c):
+        gh, gl = gauss(nn(ytn[pl.ds(pl.multiple_of(v * 256, 256), 512), :], xn[v]))
+        b = jnp.concatenate([chn[2 * v + i] for i in range(4)], axis=1)
+        nr[:, pl.ds(pl.multiple_of(v * 256, 256), 256)] = folded(nn(b, gh) + nn(b, gl))
+        return c
+
+    lax.fori_loop(0, 8, near_unit, 0, unroll=2)
 
     for o in range(3):
         quad_copies[o].wait_send()
@@ -303,7 +323,7 @@
 
     lax.fori_loop(1, quads, root_send, 0)
 
-    lax.fori_loop(16, 32, near_unit, 0)
+    lax.fori_loop(8, 16, near_unit, 0, unroll=2)
 
     def level_source(slab, q_class, values, rows):
         cls = (4 * q_class + (iota((32, LANES), 1) >> 5)) % 32
@@ -313,17 +333,23 @@
         ytc[pl.ds(at, LANES), :] = nt(eye_ref[...], f.astype(BF16)).astype(BF16)
         chc[slab] = stacked(values)
 
-    def level_prep(u, c):
-        q = jnp.where(u >= 5, u - 5, jnp.where(u >= 1, u - 1, 0))
-        slab = jnp.where(u >= 5, 0, jnp.where(u >= 1, 20, 28)) + 2 + q
-        x = pa[pl.ds(pl.multiple_of(u * 8, 8), 8), :]
-        level_source(slab, q + 2, coef3[u], source_rows(x))
+    def level_prep(w, c):
+        q = jnp.where(w < 8, 2 * w, 2 * w - 16)
+        u = q + jnp.where(w < 8, 5, 1)
+        slab = q + jnp.where(w < 8, 2, 22)
+        xs = [pa[pl.ds(pl.multiple_of((u + i) * 8, 8), 8), :] for i in range(2)]
+        for i in range(2):
+            level_source(slab + i, q + 2 + i, coef3[u + i], source_rows(xs[i]))
         bias = pltpu.roll(pltpu.roll(clb[...], (LANES - 4 * u) % LANES, axis=1), (4 * q) % 32, axis=0)
-        bias = nn(bias.astype(BF16), sel4)
-        xc[u] = jnp.concatenate([*target_stack(target_rows(x)), bias], axis=0).astype(BF16)
-        return c
-
-    lax.fori_loop(0, 21, level_prep, 0)
+        bias = nn(bias.astype(BF16), sel8)
+        xs = target_rows(jnp.concatenate(xs, axis=1))
+        xc[w] = jnp.concatenate([*target_stack(xs), bias], axis=0).astype(BF16)
+        return c
+
+    lax.fori_loop(0, 10, level_prep, 0, unroll=2)
+    level_source(30, 2, coef3[0], source_rows(pa[0:8, :]))
+    bias = nn(c1b.astype(BF16), sel8[:, 0:LANES])
+    xc1[...] = jnp.concatenate([*target_stack(target_rows(pa[0:8, :])), bias], axis=0).astype(BF16)
     for c in level_copies:
         c.wait()
     for i in range(2):
@@ -333,16 +359,21 @@
     for i, blk in ((0, r1[0]), (1, rlr[0, 4]), (3, rlr[1, 4]), (4, r1[1])):
         level_source(28 + i, i, blk[0:16], blk[16:24])
 
-    def couple_unit(u, c):
-        q = jnp.where(u >= 5, u - 5, jnp.where(u >= 1, u - 1, 0))
-        slab = jnp.where(u >= 5, 0, jnp.where(u >= 1, 20, 28)) + q
-        at = pl.multiple_of(slab * LANES, LANES)
-        gh, gl = gauss(nn(ytc[pl.ds(at, 5 * LANES), :], xc[u]))
-        v = jnp.concatenate([chc[slab + i] for i in range(5)], axis=1)
-        fc[u] = folded(nn(v, gh) + nn(v, gl))
-        return c
-
-    lax.fori_loop(0, 21, couple_unit, 0)
+    def couple_unit(w, c):
+        q = jnp.where(w < 8, 2 * w, 2 * w - 16)
+        u = q + jnp.where(w < 8, 5, 1)
+        slab = q + jnp.where(w < 8, 0, 20)
+        gh, gl = gauss(nn(ytc[pl.ds(pl.multiple_of(slab * LANES, LANES), 6 * LANES), :], xc[w]))
+        b = jnp.concatenate([chc[slab + i] for i in range(6)], axis=1)
+        g = folded(nn(b, gh) + nn(b, gl))
+        fc[u] = g[:, 0:LANES]
+        fc[u + 1] = g[:, LANES:256]
+        return c
+
+    lax.fori_loop(0, 10, couple_unit, 0, unroll=2)
+    gh, gl = gauss(nn(ytc[28 * LANES : 33 * LANES, :], xc1[...]))
+    b = jnp.concatenate([chc[28 + i] for i in range(5)], axis=1)
+    fc[0] = folded(nn(b, gh) + nn(b, gl))
 
     froot = jnp.concatenate(target_stack(target_rows(pa[21 * 8 : 22 * 8, :])), axis=0)
     troot = nt(eye_ref[0:32, :], froot.astype(BF16)).astype(BF16)
@@ -358,30 +389,26 @@
         gh, gl = gauss(nn(troot, f.astype(BF16)) + rb[pl.ds(u, 1), :])
         return acc + nt(stacked(rg[u, 0:16, :]), jnp.concatenate([gh, gl], axis=0))
 
-    acc = lax.fori_loop(0, quads, root_unit, jnp.zeros((32, 64), F32))
+    acc = lax.fori_loop(0, quads, root_unit, jnp.zeros((32, 64), F32), unroll=min(4, quads))
     acc = folded(acc)
     f0 = jnp.concatenate([acc, jnp.zeros((16, 64), F32)], axis=1)
 
     def down(f, u):
         b = stacked(f)
-        fc[u] += folded(nt(b, tbh[u]) + nt(b, tbl[u]))
-
-    down(f0, 0)
-    f1 = fc[0]
+        return fc[u] + folded(nt(b, tbh[u]) + nt(b, tbl[u]))
+
+    f1 = down(f0, 0)
     for q in range(4):
-        down(f1, 1 + q)
+        fd[q] = down(f1, 1 + q)
 
     def far(q, c):
-        down(fc[1 + q // 4], 5 + q)
+        at = pl.ds(pl.multiple_of(q * 256, 256), 256)
         bh, bl = basis_parts(q)
-        b = stacked(fc[5 + q])
-        out_ref[:, pl.ds(pl.multiple_of(q * 256, 256), 256)] += folded(nn(b, bh) + nn(b, bl))
-        return c
-
-    lax.fori_loop(0, 16, far, 0)
-
-    for c in near_copies[:0]:
-        c.wait()
+        b = stacked(down(fd[q // 4], 5 + q))
+        out_ref[:, at] = nr[:, at] + folded(nn(b, bh) + nn(b, bl))
+        return c
+
+    lax.fori_loop(0, 16, far, 0, unroll=4)
 
     def root_done(o, c):
         root_copy(o, quad).wait_send()
@@ -395,7 +422,11 @@
     if n_dev < LANES:
         rlist = jnp.pad(rlist, ((0, 0), (0, LANES - n_dev)))
     quads = n_dev // 4
+    ins = [(3, 4096), (16, 4096), (32, 4096), (32, 32, 84), (3, 32, 85), (5, 64), (20, 84), (1, LANES)]
     scratch = [
+        *[pltpu.VMEM(shape, F32 if i < 5 else jnp.int32) for i, shape in enumerate(ins)],
+        pltpu.SemaphoreType.DMA((8,)),
+        pltpu.VMEM((16, 4096), F32),
         pltpu.VMEM((8, 4096), F32),
         pltpu.VMEM((192, LANES), F32),
         pltpu.VMEM((84 * 32, LANES), F32),
@@ -405,15 +436,17 @@
         pltpu.VMEM((LANES, 256), BF16),
         pltpu.VMEM((34 * LANES, KN), BF16),
         pltpu.VMEM((34, 32, LANES), BF16),
-        pltpu.VMEM((32, KN, LANES), BF16),
+        pltpu.VMEM((16, KN, 256), BF16),
         pltpu.VMEM((33 * LANES, KC), BF16),
         pltpu.VMEM((33, 32, LANES), BF16),
-        pltpu.VMEM((21, KC, LANES), BF16),
+        pltpu.VMEM((10, KC, 256), BF16),
+        pltpu.VMEM((KC, LANES), BF16),
         pltpu.VMEM((32, LANES), F32),
         pltpu.VMEM((8, LANES), F32),
         pltpu.VMEM((32, LANES), F32),
         pltpu.VMEM((21, 16, LANES), F32),
         pltpu.VMEM((21, 16, LANES), F32),
+        pltpu.VMEM((4, 16, LANES), F32),
         pltpu.VMEM((2, 24, LANES), F32),
         pltpu.VMEM((2, 24, LANES), F32),
         pltpu.VMEM((2, 5, 24, LANES), F32),
@@ -432,7 +465,7 @@
     return pl.pallas_call(
         functools.partial(kernel, n_dev),
         out_shape=jax.ShapeDtypeStruct(rhs.shape, F32),
-        in_specs=[vmem] * 8,
+        in_specs=[pl.BlockSpec(memory_space=pltpu.HBM)] * 8,
         out_specs=vmem,
         scratch_shapes=scratch,
         compiler_params=pltpu.CompilerParams(

time: 72.5 us -> 44.5 us (0.61)
  Pallas kernels: 64.2 us -> 36.7 us
    pallas_call x1, Pallas kernels: 64.2 us -> 36.7 us  [body(): pl.pallas_call(functools.partial(kernel, n_dev), out_shape=jax.ShapeDtype...]
where the time goes in v2:
time: 44.5 us; the launch traced here: 44.1 us
  Pallas kernels  36.7 us (82%)
  local copies, waits for them, and re-layouts  7.42 us (17%)
    pallas_call x1, Pallas kernels, body(): pl.pallas_call(functools.partial(kernel, n_dev), out_shape=jax.ShapeDtype...  36.7 us
    unnamed x17, local copies, waits for them, and re-layouts  7.42 us

profile of v2, /device:TPU:0, one launch (start us, length us, event | category | flops | bytes accessed | tf_op | source)
XLA Modules:
  0.0 44.1 jit_solution(16692011227805367367)
XLA Ops:
  0.0 0.0 copy-start.7
  0.0 0.7 %copy-done.7 = s32[1,128]{1,0:T(1,128)S(1)} copy-done((s32[1,128]{1,0:T(1,128)S(1)}, s32[1,128]{1,0:T(1,128)}, u32[]{:S(2)}) %copy-start.7) | copy-done | bytes 536
  0.7 0.0 copy-start
  0.7 1.0 %copy-done = f32[32,4096]{1,0:T(8,128)S(1)} copy-done((f32[32,4096]{1,0:T(8,128)S(1)}, f32[32,4096]{1,0:T(8,128)}, u32[]{:S(2)}) %copy-start) | copy-done | bytes 524312
  1.7 0.0 copy-start.1
  1.7 1.0 %copy-done.1 = f32[32,32,84]{2,1,0:T(8,128)S(1)} copy-done((f32[32,32,84]{2,1,0:T(8,128)S(1)}, f32[32,32,84]{2,1,0:T(8,128)}, u32[]{:S(2)}) %copy-start.1) | copy-done | bytes 344088
  2.7 0.0 copy-start.2
  2.7 0.9 %copy-done.2 = f32[16,4096]{1,0:T(8,128)S(1)} copy-done((f32[16,4096]{1,0:T(8,128)S(1)}, f32[16,4096]{1,0:T(8,128)}, u32[]{:S(2)}) %copy-start.2) | copy-done | bytes 262168
  3.7 0.0 copy-start.3
  3.7 0.8 %copy-done.3 = f32[3,4096]{1,0:T(4,128)S(1)} copy-done((f32[3,4096]{1,0:T(4,128)S(1)}, f32[3,4096]{1,0:T(4,128)}, u32[]{:S(2)}) %copy-start.3) | copy-done | bytes 49176
  4.5 0.0 copy-start.4
  4.5 0.8 %copy-done.4 = f32[3,32,85]{2,1,0:T(8,128)S(1)} copy-done((f32[3,32,85]{2,1,0:T(8,128)S(1)}, f32[3,32,85]{2,1,0:T(8,128)}, u32[]{:S(2)}) %copy-start.4) | copy-done | bytes 32664
  5.3 0.0 copy-start.5
  5.3 0.7 %copy-done.5 = s32[84,20]{0,1:T(8,128)S(1)} copy-done((s32[84,20]{0,1:T(8,128)S(1)}, s32[84,20]{0,1:T(8,128)}, u32[]{:S(2)}) %copy-start.5) | copy-done | bytes 6744
  6.0 0.0 copy-start.6
  6.0 0.7 %copy-done.6 = s32[64,5]{0,1:T(8,128)S(1)} copy-done((s32[64,5]{0,1:T(8,128)S(1)}, s32[64,5]{0,1:T(8,128)}, u32[]{:S(2)}) %copy-start.6) | copy-done | bytes 1304
  6.7 36.7 %hmatvec.1 = f32[16,4096]{1,0:T(8,128)S(1)} custom-call(f32[3,4096]{1,0:T(4,128)S(1)} %copy-done.3, f32[16,4096]{1,0:T(8,128)S(1)} %copy-done.2, f32[32,4096]{1,0:T(8,128)S(1)} %copy-done, f32[32,32,84]{2,1,0:T(8,128)S(1)} %copy-done.1, f32[3,32,85]{2,1,0:T(8,128)S(1)} %copy-done.4, s32[5,64]{1,0:T(8,128)S(1)} %bitcast.3, s32[20,84]{1,0:T(8,128)S(1)} %bitcast.2, ...), custom_call_target="tpu_custom_call" | custom-call | tf_op jit(solution)/shard_map/hmatvec/pallas_call | solution.py:465
  43.4 0.7 %copy.10 = f32[16,4096]{1,0:T(8,128)} copy(f32[16,4096]{1,0:T(8,128)S(1)} %hmatvec.1) | data formatting | bytes 524288
Async XLA Ops:
  0.0 0.7 %copy-start.7 = (s32[1,128]{1,0:T(1,128)S(1)}, s32[1,128]{1,0:T(1,128)}, u32[]{:S(2)}) copy-start(s32[1,128]{1,0:T(1,128)} %rl_hbm.1) | copy-start | bytes 1540
  0.7 1.0 %copy-start = (f32[32,4096]{1,0:T(8,128)S(1)}, f32[32,4096]{1,0:T(8,128)}, u32[]{:S(2)}) copy-start(f32[32,4096]{1,0:T(8,128)} %basis_hbm.1) | copy-start | bytes 1572868
  1.7 1.0 %copy-start.1 = (f32[32,32,84]{2,1,0:T(8,128)S(1)}, f32[32,32,84]{2,1,0:T(8,128)}, u32[]{:S(2)}) copy-start(f32[32,32,84]{2,1,0:T(8,128)} %tr_hbm.1) | copy-start | bytes 1032196
  2.7 0.9 %copy-start.2 = (f32[16,4096]{1,0:T(8,128)S(1)}, f32[16,4096]{1,0:T(8,128)}, u32[]{:S(2)}) copy-start(f32[16,4096]{1,0:T(8,128)} %rhs_hbm.1) | copy-start | bytes 786436
  3.7 0.8 %copy-start.3 = (f32[3,4096]{1,0:T(4,128)S(1)}, f32[3,4096]{1,0:T(4,128)}, u32[]{:S(2)}) copy-start(f32[3,4096]{1,0:T(4,128)} %pts_hbm.1) | copy-start | bytes 147460
  4.5 0.8 %copy-start.4 = (f32[3,32,85]{2,1,0:T(8,128)S(1)}, f32[3,32,85]{2,1,0:T(8,128)}, u32[]{:S(2)}) copy-start(f32[3,32,85]{2,1,0:T(8,128)} %px_hbm.1) | copy-start | bytes 97924
  5.3 0.7 %copy-start.5 = (s32[84,20]{0,1:T(8,128)S(1)}, s32[84,20]{0,1:T(8,128)}, u32[]{:S(2)}) copy-start(s32[84,20]{0,1:T(8,128)} %param.14) | copy-start | bytes 20164
  6.0 0.7 %copy-start.6 = (s32[64,5]{0,1:T(8,128)S(1)}, s32[64,5]{0,1:T(8,128)}, u32[]{:S(2)}) copy-start(s32[64,5]{0,1:T(8,128)} %param.13) | copy-start | bytes 3844

commit v3 on v2

--- a/solution.py
+++ b/solution.py
@@ -72,6 +72,10 @@
 def target_stack(rows):
     h, m, l = thirds(rows)
     return [h, h, h, m, m, l]
+
+
+def once(fn):
+    fn()
 
 
 def gauss(e):
@@ -87,7 +91,7 @@
     nr, p8, pa, tb, tbh, tbl, eye_ref, bmask,
     ytn, chn, xn, ytc, chc, xc, xc1, clb, nlb, rb,
     gc, fc, fd,
-    sn, rn, sl, rlr, s1, r1, sq, rq, rg,
+    sn, rn, sl, rlr, s1, r1, sq, sq2, rq, rg,
     sem_s, sem_r, gs_sem, gr_sem,
 ):
     loads = {
@@ -120,8 +124,11 @@
 
     lax.fori_loop(1, quads, greet, 0)
 
-    eye_ref[...] = jnp.where(iota((LANES, LANES), 0) == iota((LANES, LANES), 1), 1.0, 0.0).astype(BF16)
-    bmask[...] = jnp.where(iota((LANES, 256), 0) // 32 == iota((LANES, 256), 1) // 64, 1.0, 0.0).astype(BF16)
+    def sec_const():
+        eye_ref[...] = jnp.where(iota((LANES, LANES), 0) == iota((LANES, LANES), 1), 1.0, 0.0).astype(BF16)
+        bmask[...] = jnp.where(iota((LANES, 256), 0) // 32 == iota((LANES, 256), 1) // 64, 1.0, 0.0).astype(BF16)
+
+    once(sec_const)
 
     loads["tr"].wait()
     lane_n, row_n = iota((LANES, 84), 1), iota((LANES, 84), 0)
@@ -146,19 +153,22 @@
     lax.fori_loop(0, 21, part, 0, unroll=3)
 
     loads["px"].wait()
-    pick = jnp.where(
-        ((iota((24, 85), 1) >= 1) & ((iota((24, 85), 1) - 1) >> 2 == iota((24, 85), 0)))
-        | ((iota((24, 85), 1) == 0) & (iota((24, 85), 0) == 21)), 1.0, 0.0).astype(BF16)
-    lane_p, row_p = iota((LANES, 85), 1), iota((LANES, 85), 0)
-    pmask = (lane_p == 0) | ((lane_p + 3) % 4 == (row_p >> 5))
-    pa[...] = jnp.zeros_like(pa)
-    for ax in range(3):
-        w = (px_ref[ax] - 0.5) * SCALE
-        w = jnp.where(pmask, jnp.concatenate([w, w, w, w], axis=0), 0.0)
-        h, m, l = thirds(w)
-        pa[pl.ds(ax, 24, stride=8), :] = (
-            nt(pick, h.astype(BF16)) + nt(pick, m.astype(BF16)) + nt(pick, l.astype(BF16))
-        )
+    def sec_prox():
+        pick = jnp.where(
+            ((iota((24, 85), 1) >= 1) & ((iota((24, 85), 1) - 1) >> 2 == iota((24, 85), 0)))
+            | ((iota((24, 85), 1) == 0) & (iota((24, 85), 0) == 21)), 1.0, 0.0).astype(BF16)
+        lane_p, row_p = iota((LANES, 85), 1), iota((LANES, 85), 0)
+        pmask = (lane_p == 0) | ((lane_p + 3) % 4 == (row_p >> 5))
+        pa[...] = jnp.zeros_like(pa)
+        for ax in range(3):
+            w = (px_ref[ax] - 0.5) * SCALE
+            w = jnp.where(pmask, jnp.concatenate([w, w, w, w], axis=0), 0.0)
+            h, m, l = thirds(w)
+            pa[pl.ds(ax, 24, stride=8), :] = (
+                nt(pick, h.astype(BF16)) + nt(pick, m.astype(BF16)) + nt(pick, l.astype(BF16))
+            )
+
+    once(sec_prox)
 
     def basis_parts(q):
         hi, lo = halves(basis_ref[:, pl.ds(q * 256, 256)])
@@ -180,19 +190,22 @@
 
     lax.fori_loop(0, 16, leaf_coef, 0, unroll=4)
 
-    for r in range(4):
+    def sec_up():
+        for r in range(4):
+            acc = jnp.zeros((32, LANES), F32)
+            for i in range(4):
+                b = stacked(coef3[5 + 4 * r + i])
+                acc += nn(b, tbh[5 + 4 * r + i]) + nn(b, tbl[5 + 4 * r + i])
+            coef3[1 + r] = folded(acc)
         acc = jnp.zeros((32, LANES), F32)
         for i in range(4):
-            b = stacked(coef3[5 + 4 * r + i])
-            acc += nn(b, tbh[5 + 4 * r + i]) + nn(b, tbl[5 + 4 * r + i])
-        coef3[1 + r] = folded(acc)
-    acc = jnp.zeros((32, LANES), F32)
-    for i in range(4):
-        b = stacked(coef3[1 + i])
-        acc += nn(b, tbh[1 + i]) + nn(b, tbl[1 + i])
-    coef3[0] = folded(acc)
-    b = stacked(coef3[0])
-    coef0 = folded(nn(b, tbh[0]) + nn(b, tbl[0]))
+            b = stacked(coef3[1 + i])
+            acc += nn(b, tbh[1 + i]) + nn(b, tbl[1 + i])
+        coef3[0] = folded(acc)
+        b = stacked(coef3[0])
+        sq[0:16, :] = folded(nn(b, tbh[0]) + nn(b, tbl[0]))
+
+    once(sec_up)
 
     pl.semaphore_wait(barrier, 7 + quads - 1)
 
@@ -202,14 +215,17 @@
             device_id=(d,), device_id_type=MESH,
         )
 
-    sq[0:16, :] = coef0
-    sq[16:24, :] = source_rows(pa[21 * 8 : 22 * 8, :])
-    for i, (to_left, to_right) in enumerate(((5, 19), (6, 20), (1, 3), (2, 4), (0, 0))):
-        for side, u in ((0, to_left), (1, to_right)):
-            sl[side, i, 0:16, :] = coef3[u]
-            sl[side, i, 16:24, :] = source_rows(pa[u * 8 : u * 8 + 8, :])
-    s1[0:16, :] = coef3[0]
-    s1[16:24, :] = source_rows(pa[0:8, :])
+    def sec_pack():
+        sq[16:24, :] = source_rows(pa[21 * 8 : 22 * 8, :])
+        for i, (to_left, to_right) in enumerate(((5, 19), (6, 20), (1, 3), (2, 4), (0, 0))):
+            for side, u in ((0, to_left), (1, to_right)):
+                sl[side, i, 0:16, :] = coef3[u]
+                sl[side, i, 16:24, :] = source_rows(pa[u * 8 : u * 8 + 8, :])
+        s1[0:16, :] = coef3[0]
+        s1[16:24, :] = source_rows(pa[0:8, :])
+
+    once(sec_pack)
+
     rq[seat] = sq[...]
     quad_copies = [
         pltpu.make_async_remote_copy(
@@ -284,10 +300,6 @@
         return c
 
     lax.fori_loop(0, 16, near_prep, 0, unroll=4)
-    for c in near_copies:
-        c.wait()
-    near_source(0, rn[0, 0:16, :], rn[0, 16:24, :])
-    near_source(33, rn[1, 0:16, :], rn[1, 16:24, :])
 
     def near_unit(v, c):
         gh, gl = gauss(nn(ytn[pl.ds(pl.multiple_of(v * 256, 256), 512), :], xn[v]))
@@ -295,7 +307,7 @@
         nr[:, pl.ds(pl.multiple_of(v * 256, 256), 256)] = folded(nn(b, gh) + nn(b, gl))
         return c
 
-    lax.fori_loop(0, 8, near_unit, 0, unroll=2)
+    lax.fori_loop(1, 7, near_unit, 0, unroll=2)
 
     for o in range(3):
         quad_copies[o].wait_send()
@@ -307,13 +319,12 @@
         ).wait_recv()
     group = iota((24, LANES), 1) >> 5
     merged = jnp.where(group == 0, rq[0], jnp.where(group == 1, rq[1], jnp.where(group == 2, rq[2], rq[3])))
-    sq2 = sn
-    sq2[0] = merged
+    sq2[...] = merged
     rg[quad] = merged
 
     def root_copy(o, slot):
         return pltpu.make_async_remote_copy(
-            src_ref=sq2.at[0], dst_ref=rg.at[slot], send_sem=gs_sem.at[o], recv_sem=gr_sem.at[slot],
+            src_ref=sq2, dst_ref=rg.at[slot], send_sem=gs_sem.at[o], recv_sem=gr_sem.at[slot],
             device_id=(dst(o),), device_id_type=MESH,
         )
 
@@ -323,7 +334,7 @@
 
     lax.fori_loop(1, quads, root_send, 0)
 
-    lax.fori_loop(8, 16, near_unit, 0, unroll=2)
+    lax.fori_loop(7, 15, near_unit, 0, unroll=2)
 
     def level_source(slab, q_class, values, rows):
         cls = (4 * q_class + (iota((32, LANES), 1) >> 5)) % 32
@@ -352,12 +363,15 @@
     xc1[...] = jnp.concatenate([*target_stack(target_rows(pa[0:8, :])), bias], axis=0).astype(BF16)
     for c in level_copies:
         c.wait()
-    for i in range(2):
-        for first, k, n in ((0, 0, 16), (20, 2, 4)):
-            level_source(first + i, i, rlr[0, k + i, 0:16, :], rlr[0, k + i, 16:24, :])
-            level_source(first + 2 + n + i, 2 + n + i, rlr[1, k + i, 0:16, :], rlr[1, k + i, 16:24, :])
-    for i, blk in ((0, r1[0]), (1, rlr[0, 4]), (3, rlr[1, 4]), (4, r1[1])):
-        level_source(28 + i, i, blk[0:16], blk[16:24])
+    def sec_halo():
+        for i in range(2):
+            for first, k, n in ((0, 0, 16), (20, 2, 4)):
+                level_source(first + i, i, rlr[0, k + i, 0:16, :], rlr[0, k + i, 16:24, :])
+                level_source(first + 2 + n + i, 2 + n + i, rlr[1, k + i, 0:16, :], rlr[1, k + i, 16:24, :])
+        for i, blk in ((0, r1[0]), (1, rlr[0, 4]), (3, rlr[1, 4]), (4, r1[1])):
+            level_source(28 + i, i, blk[0:16], blk[16:24])
+
+    once(sec_halo)
 
     def couple_unit(w, c):
         q = jnp.where(w < 8, 2 * w, 2 * w - 16)
@@ -371,9 +385,20 @@
         return c
 
     lax.fori_loop(0, 10, couple_unit, 0, unroll=2)
-    gh, gl = gauss(nn(ytc[28 * LANES : 33 * LANES, :], xc1[...]))
-    b = jnp.concatenate([chc[28 + i] for i in range(5)], axis=1)
-    fc[0] = folded(nn(b, gh) + nn(b, gl))
+    def sec_l1():
+        gh, gl = gauss(nn(ytc[28 * LANES : 33 * LANES, :], xc1[...]))
+        b = jnp.concatenate([chc[28 + i] for i in range(5)], axis=1)
+        fc[0] = folded(nn(b, gh) + nn(b, gl))
+
+    once(sec_l1)
+
+    for c in near_copies:
+        c.wait()
+    near_source(0, rn[0, 0:16, :], rn[0, 16:24, :])
+    near_source(33, rn[1, 0:16, :], rn[1, 16:24, :])
+
+    near_unit(0, 0)
+    near_unit(15, 0)
 
     froot = jnp.concatenate(target_stack(target_rows(pa[21 * 8 : 22 * 8, :])), axis=0)
     troot = nt(eye_ref[0:32, :], froot.astype(BF16)).astype(BF16)
@@ -384,31 +409,48 @@
 
     lax.fori_loop(1, quads, root_wait, 0)
 
-    def root_unit(u, acc):
-        f = jnp.concatenate(source_stack(rg[u, 16:24, :]), axis=0)
-        gh, gl = gauss(nn(troot, f.astype(BF16)) + rb[pl.ds(u, 1), :])
-        return acc + nt(stacked(rg[u, 0:16, :]), jnp.concatenate([gh, gl], axis=0))
-
-    acc = lax.fori_loop(0, quads, root_unit, jnp.zeros((32, 64), F32), unroll=min(4, quads))
-    acc = folded(acc)
-    f0 = jnp.concatenate([acc, jnp.zeros((16, 64), F32)], axis=1)
-
-    def down(f, u):
-        b = stacked(f)
-        return fc[u] + folded(nt(b, tbh[u]) + nt(b, tbl[u]))
-
-    f1 = down(f0, 0)
-    for q in range(4):
-        fd[q] = down(f1, 1 + q)
+    def sec_tail():
+        batch = min(8, quads)
+
+        def root_unit(i, acc):
+            us = [i * batch + j for j in range(batch)]
+            rows = jnp.concatenate([rg[u, 16:24, :] for u in us], axis=1)
+            f = jnp.concatenate(source_stack(rows), axis=0).astype(BF16)
+            bias = jnp.concatenate([rb[pl.ds(u, 1), :] for u in us], axis=1)
+            gh, gl = gauss(nn(troot, f) + bias)
+            v = stacked(jnp.concatenate([rg[u, 0:16, :] for u in us], axis=1))
+            return acc + nt(v, jnp.concatenate([gh, gl], axis=0))
+
+        acc = jnp.zeros((32, 64), F32)
+        for i in range(quads // batch):
+            acc = root_unit(i, acc)
+        acc = folded(acc)
+        f0 = jnp.concatenate([acc, jnp.zeros((16, 64), F32)], axis=1)
+
+        def down(f, u):
+            b = stacked(f)
+            return fc[u] + folded(nt(b, tbh[u]) + nt(b, tbl[u]))
+
+        f1 = stacked(down(f0, 0))
+        w = [t[1:5].reshape(512, LANES) for t in (tbh, tbl)]
+        f2 = folded(nt(f1, w[0]) + nt(f1, w[1]))
+        for r in range(4):
+            b = stacked(fc[1 + r] + f2[:, r * LANES : (r + 1) * LANES])
+            w = [t[5 + 4 * r : 9 + 4 * r].reshape(512, LANES) for t in (tbh, tbl)]
+            f3 = folded(nt(b, w[0]) + nt(b, w[1]))
+            for i in range(4):
+                fd[4 * r + i] = stacked(fc[5 + 4 * r + i] + f3[:, i * LANES : (i + 1) * LANES])
+
+    once(sec_tail)
 
     def far(q, c):
         at = pl.ds(pl.multiple_of(q * 256, 256), 256)
         bh, bl = basis_parts(q)
-        b = stacked(down(fd[q // 4], 5 + q))
+        b = fd[q]
         out_ref[:, at] = nr[:, at] + folded(nn(b, bh) + nn(b, bl))
         return c
 
-    lax.fori_loop(0, 16, far, 0, unroll=4)
+    lax.fori_loop(0, 16, far, 0, unroll=8)
 
     def root_done(o, c):
         root_copy(o, quad).wait_send()
@@ -446,13 +488,14 @@
         pltpu.VMEM((32, LANES), F32),
         pltpu.VMEM((21, 16, LANES), F32),
         pltpu.VMEM((21, 16, LANES), F32),
-        pltpu.VMEM((4, 16, LANES), F32),
+        pltpu.VMEM((16, 32, LANES), BF16),
         pltpu.VMEM((2, 24, LANES), F32),
         pltpu.VMEM((2, 24, LANES), F32),
         pltpu.VMEM((2, 5, 24, LANES), F32),
         pltpu.VMEM((2, 5, 24, LANES), F32),
         pltpu.VMEM((24, LANES), F32),
         pltpu.VMEM((2, 24, LANES), F32),
+        pltpu.VMEM((24, LANES), F32),
         pltpu.VMEM((24, LANES), F32),
         pltpu.VMEM((4, 24, LANES), F32),
         pltpu.VMEM((quads, 24, LANES), F32),
@@ -469,7 +512,7 @@
         out_specs=vmem,
         scratch_shapes=scratch,
         compiler_params=pltpu.CompilerParams(
-            collective_id=0, has_side_effects=True, vmem_limit_bytes=40 * 2**20
+            collective_id=0, has_side_effects=True, vmem_limit_bytes=60 * 2**20
         ),
         name="hmatvec",
     )(points, rhs, leaf_basis, transfer, proxies, near_list.T, couple_list.T, rlist)

time: 44.5 us -> 28.1 us (0.63)
  Pallas kernels: 36.7 us -> 25.9 us
  local copies, waits for them, and re-layouts: 7.42 us -> 1.67 us
    pallas_call x1, Pallas kernels: 36.7 us -> 25.9 us  [body(): pl.pallas_call(functools.partial(kernel, n_dev), out_shape=jax.ShapeDtype...]
    unnamed x17 -> x1, local copies, waits for them, and re-layouts: 7.42 us -> 1.67 us
where the time goes in v3:
time: 28.1 us; the launch traced here: 27.6 us
  Pallas kernels  25.9 us (92%)
  local copies, waits for them, and re-layouts  1.67 us (6%)
    pallas_call x1, Pallas kernels, body(): pl.pallas_call(functools.partial(kernel, n_dev), out_shape=jax.ShapeDtype...  25.9 us
    unnamed x1, local copies, waits for them, and re-layouts  1.67 us

profile of v3, /device:TPU:0, one launch (start us, length us, event | category | flops | bytes accessed | tf_op | source)
XLA Modules:
  0.0 27.6 jit_solution(6920378596237397100)
XLA Ops:
  0.0 25.9 %hmatvec.1 = f32[16,4096]{1,0:T(8,128)} custom-call(f32[3,4096]{1,0:T(4,128)} %pts_hbm.1, f32[16,4096]{1,0:T(8,128)} %rhs_hbm.1, f32[32,4096]{1,0:T(8,128)} %basis_hbm.1, f32[32,32,84]{2,1,0:T(8,128)} %tr_hbm.1, f32[3,32,85]{2,1,0:T(8,128)} %px_hbm.1, s32[5,64]{1,0:T(8,128)} %bitcast.3, s32[20,84]{1,0:T(8,128)} %bitcast.2, s32[1,128]{1,0:T(1,128)} %rl_hbm.1), custom_call_target="tpu_custom_call" | custom-call | tf_op jit(solution)/shard_map/hmatvec/pallas_call | solution.py:508
  25.9 1.7 %copy.10 = f32[16,4096]{1,0:T(8,128)} copy(f32[16,4096]{1,0:T(8,128)} %hmatvec.1) | data formatting | bytes 524288

commit v4 on v3

--- a/solution.py
+++ b/solution.py
@@ -97,8 +97,8 @@
     loads = {
         name: pltpu.make_async_copy(src, dst, in_sem.at[i])
         for i, (name, src, dst) in enumerate((
-            ("tr", tr_hbm, tr_ref), ("px", px_hbm, px_ref), ("basis", basis_hbm, basis_ref),
-            ("rhs", rhs_hbm, rhs_ref), ("pts", pts_hbm, pts_ref), ("nl", nl_hbm, nl_ref),
+            ("px", px_hbm, px_ref), ("basis", basis_hbm, basis_ref), ("rhs", rhs_hbm, rhs_ref),
+            ("tr", tr_hbm, tr_ref), ("pts", pts_hbm, pts_ref), ("nl", nl_hbm, nl_ref),
             ("cl", cl_hbm, cl_ref), ("rl", rl_hbm, rl_ref),
         ))
     }
@@ -129,28 +129,6 @@
         bmask[...] = jnp.where(iota((LANES, 256), 0) // 32 == iota((LANES, 256), 1) // 64, 1.0, 0.0).astype(BF16)
 
     once(sec_const)
-
-    loads["tr"].wait()
-    lane_n, row_n = iota((LANES, 84), 1), iota((LANES, 84), 0)
-    tmask = (lane_n < 4) | (((lane_n >> 2) + 3) % 4 == (row_n >> 5))
-    eye84 = jnp.where(iota((84, 84), 0) == iota((84, 84), 1), 1.0, 0.0).astype(BF16)
-
-    def turn(a, c):
-        w = tr_ref[a]
-        w = jnp.where(tmask, jnp.concatenate([w, w, w, w], axis=0), 0.0)
-        hi, lo = halves(w)
-        tb[pl.ds(a, 84, stride=32), :] = nt(eye84, hi) + nt(eye84, lo)
-        return c
-
-    lax.fori_loop(0, 32, turn, 0, unroll=4)
-
-    def part(i, c):
-        hi, lo = halves(tb[pl.ds(i * LANES, LANES), :])
-        tbh[i] = hi
-        tbl[i] = lo
-        return c
-
-    lax.fori_loop(0, 21, part, 0, unroll=3)
 
     loads["px"].wait()
     def sec_prox():
@@ -189,6 +167,42 @@
         return c
 
     lax.fori_loop(0, 16, leaf_coef, 0, unroll=4)
+
+    loads["tr"].wait()
+    lane_n, row_n = iota((LANES, 84), 1), iota((LANES, 84), 0)
+    tmask = (lane_n < 4) | (((lane_n >> 2) + 3) % 4 == (row_n >> 5))
+    eye88 = jnp.where(iota((88, 84), 0) == iota((88, 84), 1), 1.0, 0.0).astype(BF16)
+
+    bit = [(iota((8, LANES), 0) & k) == 0 for k in (1, 2, 4)]
+
+    def turn(g, c):
+        wide = []
+        for i in range(8):
+            w = tr_ref[8 * g + i]
+            w = jnp.where(tmask, jnp.concatenate([w, w, w, w], axis=0), 0.0)
+            hi, lo = halves(w)
+            wide.append(nt(eye88, hi) + nt(eye88, lo))
+        for n in range(0, 84, 8):
+            v = [w[n : n + 8] for w in wide]
+            for p, k in ((2, 4), (1, 2), (0, 1)):
+                for i in range(8):
+                    if not i & k:
+                        x, y = v[i], v[i + k]
+                        v[i] = jnp.where(bit[p], x, pltpu.roll(y, k, axis=0))
+                        v[i + k] = jnp.where(bit[p], pltpu.roll(x, 8 - k, axis=0), y)
+            for i in range(min(8, 84 - n)):
+                tb[pl.ds(pl.multiple_of((n + i) * 32 + 8 * g, 8), 8), :] = v[i]
+        return c
+
+    lax.fori_loop(0, 4, turn, 0, unroll=2)
+
+    def part(i, c):
+        hi, lo = halves(tb[pl.ds(i * LANES, LANES), :])
+        tbh[i] = hi
+        tbl[i] = lo
+        return c
+
+    lax.fori_loop(0, 21, part, 0, unroll=3)
 
     def sec_up():
         for r in range(4):
@@ -307,7 +321,7 @@
         nr[:, pl.ds(pl.multiple_of(v * 256, 256), 256)] = folded(nn(b, gh) + nn(b, gl))
         return c
 
-    lax.fori_loop(1, 7, near_unit, 0, unroll=2)
+    lax.fori_loop(1, 7, near_unit, 0, unroll=3)
 
     for o in range(3):
         quad_copies[o].wait_send()
@@ -334,7 +348,7 @@
 
     lax.fori_loop(1, quads, root_send, 0)
 
-    lax.fori_loop(7, 15, near_unit, 0, unroll=2)
+    lax.fori_loop(7, 15, near_unit, 0, unroll=4)
 
     def level_source(slab, q_class, values, rows):
         cls = (4 * q_class + (iota((32, LANES), 1) >> 5)) % 32
@@ -384,7 +398,7 @@
         fc[u + 1] = g[:, LANES:256]
         return c
 
-    lax.fori_loop(0, 10, couple_unit, 0, unroll=2)
+    lax.fori_loop(0, 10, couple_unit, 0, unroll=5)
     def sec_l1():
         gh, gl = gauss(nn(ytc[28 * LANES : 33 * LANES, :], xc1[...]))
         b = jnp.concatenate([chc[28 + i] for i in range(5)], axis=1)

time: 28.1 us -> 26.3 us (0.936); the launches traced: 27.6 us -> 26.1 us
  Pallas kernels: 25.9 us -> 24.4 us
    pallas_call x1, Pallas kernels: 25.9 us -> 24.4 us  [body(): pl.pallas_call(functools.partial(kernel, n_dev), out_shape=jax.ShapeDtype...]
where the time goes in v4:
time: 26.3 us; the launch traced here: 26.1 us
  Pallas kernels  24.4 us (93%)
  local copies, waits for them, and re-layouts  1.67 us (6%)
    pallas_call x1, Pallas kernels, body(): pl.pallas_call(functools.partial(kernel, n_dev), out_shape=jax.ShapeDtype...  24.4 us
    unnamed x1, local copies, waits for them, and re-layouts  1.67 us

profile of v4, /device:TPU:0, one launch (start us, length us, event | category | flops | bytes accessed | tf_op | source)
XLA Modules:
  0.0 26.1 jit_solution(8418198346572300085)
XLA Ops:
  0.0 24.4 %hmatvec.1 = f32[16,4096]{1,0:T(8,128)} custom-call(f32[3,4096]{1,0:T(4,128)} %pts_hbm.1, f32[16,4096]{1,0:T(8,128)} %rhs_hbm.1, f32[32,4096]{1,0:T(8,128)} %basis_hbm.1, f32[32,32,84]{2,1,0:T(8,128)} %tr_hbm.1, f32[3,32,85]{2,1,0:T(8,128)} %px_hbm.1, s32[5,64]{1,0:T(8,128)} %bitcast.3, s32[20,84]{1,0:T(8,128)} %bitcast.2, s32[1,128]{1,0:T(1,128)} %rl_hbm.1), custom_call_target="tpu_custom_call" | custom-call | tf_op jit(solution)/shard_map/hmatvec/pallas_call | solution.py:522
  24.4 1.7 %copy.10 = f32[16,4096]{1,0:T(8,128)} copy(f32[16,4096]{1,0:T(8,128)} %hmatvec.1) | data formatting | bytes 524288

commit v5 on v4

--- a/solution.py
+++ b/solution.py
@@ -105,14 +105,14 @@
     for c in loads.values():
         c.start()
     me = lax.axis_index("leaf")
-    quads = n_dev // 4
-    quad, seat = me // 4, me % 4
+    groups = n_dev // 8
+    group, seat = me // 8, me % 8
     left, right = (me + n_dev - 1) % n_dev, (me + 1) % n_dev
     left2, right2 = (me + n_dev - 2) % n_dev, (me + 2) % n_dev
-    peers = [quad * 4 + (seat + o) % 4 for o in range(1, 4)]
+    peers = [group * 8 + (seat + o) % 8 for o in range(1, 8)]
 
     def dst(o):
-        return ((quad + o) % quads) * 4 + seat
+        return ((group + o) % groups) * 8 + seat
 
     barrier = pltpu.get_barrier_semaphore()
     for d in [left, right, left2, right2, *peers]:
@@ -122,7 +122,7 @@
         pl.semaphore_signal(barrier, inc=1, device_id=(dst(o),), device_id_type=MESH)
         return c
 
-    lax.fori_loop(1, quads, greet, 0)
+    lax.fori_loop(1, groups, greet, 0)
 
     def sec_const():
         eye_ref[...] = jnp.where(iota((LANES, LANES), 0) == iota((LANES, LANES), 1), 1.0, 0.0).astype(BF16)
@@ -166,11 +166,11 @@
         coef3[5 + q] = folded(nt(v, bh) + nt(v, bl))
         return c
 
-    lax.fori_loop(0, 16, leaf_coef, 0, unroll=4)
 
     loads["tr"].wait()
     lane_n, row_n = iota((LANES, 84), 1), iota((LANES, 84), 0)
     tmask = (lane_n < 4) | (((lane_n >> 2) + 3) % 4 == (row_n >> 5))
+    tmask = jnp.where(tmask, 1.0, 0.0).astype(BF16)
     eye88 = jnp.where(iota((88, 84), 0) == iota((88, 84), 1), 1.0, 0.0).astype(BF16)
 
     bit = [(iota((8, LANES), 0) & k) == 0 for k in (1, 2, 4)]
@@ -179,8 +179,7 @@
         wide = []
         for i in range(8):
             w = tr_ref[8 * g + i]
-            w = jnp.where(tmask, jnp.concatenate([w, w, w, w], axis=0), 0.0)
-            hi, lo = halves(w)
+            hi, lo = [jnp.concatenate([x, x, x, x], axis=0) * tmask for x in halves(w)]
             wide.append(nt(eye88, hi) + nt(eye88, lo))
         for n in range(0, 84, 8):
             v = [w[n : n + 8] for w in wide]
@@ -192,6 +191,8 @@
                         v[i + k] = jnp.where(bit[p], pltpu.roll(x, 8 - k, axis=0), y)
             for i in range(min(8, 84 - n)):
                 tb[pl.ds(pl.multiple_of((n + i) * 32 + 8 * g, 8), 8), :] = v[i]
+        for i in range(4):
+            leaf_coef(4 * g + i, 0)
         return c
 
     lax.fori_loop(0, 4, turn, 0, unroll=2)
@@ -221,7 +222,7 @@
 
     once(sec_up)
 
-    pl.semaphore_wait(barrier, 7 + quads - 1)
+    pl.semaphore_wait(barrier, 11 + groups - 1)
 
     def remote(src, dst_ref, i, d):
         return pltpu.make_async_remote_copy(
@@ -230,7 +231,7 @@
         )
 
     def sec_pack():
-        sq[16:24, :] = source_rows(pa[21 * 8 : 22 * 8, :])
+        sq[16:19, :] = pa[21 * 8 : 21 * 8 + 3, :]
         for i, (to_left, to_right) in enumerate(((5, 19), (6, 20), (1, 3), (2, 4), (0, 0))):
             for side, u in ((0, to_left), (1, to_right)):
                 sl[side, i, 0:16, :] = coef3[u]
@@ -241,14 +242,14 @@
     once(sec_pack)
 
     rq[seat] = sq[...]
-    quad_copies = [
+    group_copies = [
         pltpu.make_async_remote_copy(
             src_ref=sq, dst_ref=rq.at[seat], send_sem=sem_s.at[6 + o], recv_sem=sem_r.at[6 + seat],
             device_id=(peers[o],), device_id_type=MESH,
         )
-        for o in range(3)
+        for o in range(7)
     ]
-    for c in quad_copies:
+    for c in group_copies:
         c.start()
     level_copies = [
         remote(sl.at[0], rlr.at[1], 2, left),
@@ -315,38 +316,48 @@
 
     lax.fori_loop(0, 16, near_prep, 0, unroll=4)
 
+    def chunked(feats, first, targets, values, slab, chunks):
+        acc = None
+        for i in range(chunks):
+            at = pl.ds(pl.multiple_of(first + i * 256, 256), 256)
+            gh, gl = gauss(nn(feats[at, :], targets))
+            b = jnp.concatenate([values[slab + 2 * i], values[slab + 2 * i + 1]], axis=1)
+            y = nn(b, gh) + nn(b, gl)
+            acc = y if acc is None else acc + y
+        return folded(acc)
+
     def near_unit(v, c):
-        gh, gl = gauss(nn(ytn[pl.ds(pl.multiple_of(v * 256, 256), 512), :], xn[v]))
-        b = jnp.concatenate([chn[2 * v + i] for i in range(4)], axis=1)
-        nr[:, pl.ds(pl.multiple_of(v * 256, 256), 256)] = folded(nn(b, gh) + nn(b, gl))
+        y = chunked(ytn, v * 256, xn[v], chn, 2 * v, 2)
+        nr[:, pl.ds(pl.multiple_of(v * 256, 256), 256)] = y
         return c
 
     lax.fori_loop(1, 7, near_unit, 0, unroll=3)
 
-    for o in range(3):
-        quad_copies[o].wait_send()
-    for o in range(1, 4):
-        frm = (seat + o) % 4
+    for o in range(7):
+        group_copies[o].wait_send()
+    for o in range(1, 8):
+        frm = (seat + o) % 8
         pltpu.make_async_remote_copy(
             src_ref=sq, dst_ref=rq.at[frm], send_sem=sem_s.at[6], recv_sem=sem_r.at[6 + frm],
             device_id=(left,), device_id_type=MESH,
         ).wait_recv()
-    group = iota((24, LANES), 1) >> 5
-    merged = jnp.where(group == 0, rq[0], jnp.where(group == 1, rq[1], jnp.where(group == 2, rq[2], rq[3])))
-    sq2[...] = merged
-    rg[quad] = merged
-
-    def root_copy(o, slot):
-        return pltpu.make_async_remote_copy(
-            src_ref=sq2, dst_ref=rg.at[slot], send_sem=gs_sem.at[o], recv_sem=gr_sem.at[slot],
+    place = iota((19, LANES), 1) >> 5
+    for i in range(2):
+        blocks = [rq[4 * i + j] for j in range(4)]
+        merged = blocks[3]
+        for j in range(3):
+            merged = jnp.where(place == j, blocks[j], merged)
+        sq2[i] = merged
+        rg[group, i] = merged
+
+    def root_send(o, c):
+        pltpu.make_async_remote_copy(
+            src_ref=sq2, dst_ref=rg.at[group], send_sem=gs_sem.at[0], recv_sem=gr_sem.at[0],
             device_id=(dst(o),), device_id_type=MESH,
-        )
-
-    def root_send(o, c):
-        root_copy(o, quad).start()
-        return c
-
-    lax.fori_loop(1, quads, root_send, 0)
+        ).start()
+        return c
+
+    lax.fori_loop(1, groups, root_send, 0)
 
     lax.fori_loop(7, 15, near_unit, 0, unroll=4)
 
@@ -371,7 +382,7 @@
         xc[w] = jnp.concatenate([*target_stack(xs), bias], axis=0).astype(BF16)
         return c
 
-    lax.fori_loop(0, 10, level_prep, 0, unroll=2)
+    lax.fori_loop(0, 10, level_prep, 0, unroll=5)
     level_source(30, 2, coef3[0], source_rows(pa[0:8, :]))
     bias = nn(c1b.astype(BF16), sel8[:, 0:LANES])
     xc1[...] = jnp.concatenate([*target_stack(target_rows(pa[0:8, :])), bias], axis=0).astype(BF16)
@@ -391,9 +402,7 @@
         q = jnp.where(w < 8, 2 * w, 2 * w - 16)
         u = q + jnp.where(w < 8, 5, 1)
         slab = q + jnp.where(w < 8, 0, 20)
-        gh, gl = gauss(nn(ytc[pl.ds(pl.multiple_of(slab * LANES, LANES), 6 * LANES), :], xc[w]))
-        b = jnp.concatenate([chc[slab + i] for i in range(6)], axis=1)
-        g = folded(nn(b, gh) + nn(b, gl))
+        g = chunked(ytc, slab * LANES, xc[w], chc, slab, 3)
         fc[u] = g[:, 0:LANES]
         fc[u + 1] = g[:, LANES:256]
         return c
@@ -417,26 +426,25 @@
     froot = jnp.concatenate(target_stack(target_rows(pa[21 * 8 : 22 * 8, :])), axis=0)
     troot = nt(eye_ref[0:32, :], froot.astype(BF16)).astype(BF16)
 
-    def root_wait(o, c):
-        root_copy(o, (quad + quads - o) % quads).wait_recv()
-        return c
-
-    lax.fori_loop(1, quads, root_wait, 0)
+    if groups > 1:
+        others = rg.at[pl.ds(0, groups - 1)]
+        pltpu.make_async_copy(others, others, gr_sem.at[0]).wait()
 
     def sec_tail():
-        batch = min(8, quads)
+        batch = min(8, 2 * groups)
 
         def root_unit(i, acc):
-            us = [i * batch + j for j in range(batch)]
-            rows = jnp.concatenate([rg[u, 16:24, :] for u in us], axis=1)
+            us = [(i * batch + j) // 2 for j in range(batch)]
+            rows = jnp.concatenate([rg[u, j % 2, 16:19, :] for j, u in enumerate(us)], axis=1)
+            rows = source_rows(jnp.concatenate([rows, jnp.zeros((5, rows.shape[1]), F32)], axis=0))
             f = jnp.concatenate(source_stack(rows), axis=0).astype(BF16)
-            bias = jnp.concatenate([rb[pl.ds(u, 1), :] for u in us], axis=1)
+            bias = jnp.concatenate([rb[pl.ds(i * batch + j, 1), :] for j in range(batch)], axis=1)
             gh, gl = gauss(nn(troot, f) + bias)
-            v = stacked(jnp.concatenate([rg[u, 0:16, :] for u in us], axis=1))
+            v = stacked(jnp.concatenate([rg[u, j % 2, 0:16, :] for j, u in enumerate(us)], axis=1))
             return acc + nt(v, jnp.concatenate([gh, gl], axis=0))
 
         acc = jnp.zeros((32, 64), F32)
-        for i in range(quads // batch):
+        for i in range(2 * groups // batch):
             acc = root_unit(i, acc)
         acc = folded(acc)
         f0 = jnp.concatenate([acc, jnp.zeros((16, 64), F32)], axis=1)
@@ -466,18 +474,16 @@
 
     lax.fori_loop(0, 16, far, 0, unroll=8)
 
-    def root_done(o, c):
-        root_copy(o, quad).wait_send()
-        return c
-
-    lax.fori_loop(1, quads, root_done, 0)
+    if groups > 1:
+        others = rg.at[pl.ds(0, groups - 1)]
+        pltpu.make_async_copy(others, others, gs_sem.at[0]).wait()
 
 
 def body(n_dev, points, rhs, leaf_basis, transfer, proxies, near_list, couple_list, root_list):
     rlist = root_list
     if n_dev < LANES:
         rlist = jnp.pad(rlist, ((0, 0), (0, LANES - n_dev)))
-    quads = n_dev // 4
+    groups = n_dev // 8
     ins = [(3, 4096), (16, 4096), (32, 4096), (32, 32, 84), (3, 32, 85), (5, 64), (20, 84), (1, LANES)]
     scratch = [
         *[pltpu.VMEM(shape, F32 if i < 5 else jnp.int32) for i, shape in enumerate(ins)],
@@ -509,14 +515,14 @@
         pltpu.VMEM((2, 5, 24, LANES), F32),
         pltpu.VMEM((24, LANES), F32),
         pltpu.VMEM((2, 24, LANES), F32),
-        pltpu.VMEM((24, LANES), F32),
-        pltpu.VMEM((24, LANES), F32),
-        pltpu.VMEM((4, 24, LANES), F32),
-        pltpu.VMEM((quads, 24, LANES), F32),
-        pltpu.SemaphoreType.DMA((10,)),
-        pltpu.SemaphoreType.DMA((10,)),
-        pltpu.SemaphoreType.DMA((quads,)),
-        pltpu.SemaphoreType.DMA((quads,)),
+        pltpu.VMEM((19, LANES), F32),
+        pltpu.VMEM((2, 19, LANES), F32),
+        pltpu.VMEM((8, 19, LANES), F32),
+        pltpu.VMEM((groups, 2, 19, LANES), F32),
+        pltpu.SemaphoreType.DMA((14,)),
+        pltpu.SemaphoreType.DMA((14,)),
+        pltpu.SemaphoreType.DMA((1,)),
+        pltpu.SemaphoreType.DMA((1,)),
     ]
     vmem = pl.BlockSpec(memory_space=pltpu.VMEM)
     return pl.pallas_call(

time: 26.3 us -> 24.7 us (0.939)
  Pallas kernels: 24.4 us -> 22.9 us
    pallas_call x1, Pallas kernels: 24.4 us -> 22.9 us  [body(): pl.pallas_call(functools.partial(kernel, n_dev), out_shape=jax.ShapeDtype...]
where the time goes in v5:
time: 24.7 us; the launch traced here: 24.6 us
  Pallas kernels  22.9 us (93%)
  local copies, waits for them, and re-layouts  1.67 us (7%)
    pallas_call x1, Pallas kernels, body(): pl.pallas_call(functools.partial(kernel, n_dev), out_shape=jax.ShapeDtype...  22.9 us
    unnamed x1, local copies, waits for them, and re-layouts  1.67 us

profile of v5, /device:TPU:0, one launch (start us, length us, event | category | flops | bytes accessed | tf_op | source)
XLA Modules:
  0.0 24.6 jit_solution(9190750634077747447)
XLA Ops:
  0.0 22.9 %hmatvec.1 = f32[16,4096]{1,0:T(8,128)} custom-call(f32[3,4096]{1,0:T(4,128)} %pts_hbm.1, f32[16,4096]{1,0:T(8,128)} %rhs_hbm.1, f32[32,4096]{1,0:T(8,128)} %basis_hbm.1, f32[32,32,84]{2,1,0:T(8,128)} %tr_hbm.1, f32[3,32,85]{2,1,0:T(8,128)} %px_hbm.1, s32[5,64]{1,0:T(8,128)} %bitcast.3, s32[20,84]{1,0:T(8,128)} %bitcast.2, s32[1,128]{1,0:T(1,128)} %rl_hbm.1), custom_call_target="tpu_custom_call" | custom-call | tf_op jit(solution)/shard_map/hmatvec/pallas_call | solution.py:528
  22.9 1.7 %copy.10 = f32[16,4096]{1,0:T(8,128)} copy(f32[16,4096]{1,0:T(8,128)} %hmatvec.1) | data formatting | bytes 524288

commit v6 on v5

--- a/solution.py
+++ b/solution.py
@@ -195,7 +195,7 @@
             leaf_coef(4 * g + i, 0)
         return c
 
-    lax.fori_loop(0, 4, turn, 0, unroll=2)
+    lax.fori_loop(0, 4, turn, 0, unroll=4)
 
     def part(i, c):
         hi, lo = halves(tb[pl.ds(i * LANES, LANES), :])
@@ -206,17 +206,14 @@
     lax.fori_loop(0, 21, part, 0, unroll=3)
 
     def sec_up():
+        def rise(first, to):
+            b = jnp.concatenate([stacked(coef3[first + i]) for i in range(4)], axis=1)
+            w = [t[first : first + 4].reshape(512, LANES) for t in (tbh, tbl)]
+            coef3[to] = folded(nn(b, w[0]) + nn(b, w[1]))
+
         for r in range(4):
-            acc = jnp.zeros((32, LANES), F32)
-            for i in range(4):
-                b = stacked(coef3[5 + 4 * r + i])
-                acc += nn(b, tbh[5 + 4 * r + i]) + nn(b, tbl[5 + 4 * r + i])
-            coef3[1 + r] = folded(acc)
-        acc = jnp.zeros((32, LANES), F32)
-        for i in range(4):
-            b = stacked(coef3[1 + i])
-            acc += nn(b, tbh[1 + i]) + nn(b, tbl[1 + i])
-        coef3[0] = folded(acc)
+            rise(5 + 4 * r, 1 + r)
+        rise(1, 0)
         b = stacked(coef3[0])
         sq[0:16, :] = folded(nn(b, tbh[0]) + nn(b, tbl[0]))
 
@@ -230,17 +227,7 @@
             device_id=(d,), device_id_type=MESH,
         )
 
-    def sec_pack():
-        sq[16:19, :] = pa[21 * 8 : 21 * 8 + 3, :]
-        for i, (to_left, to_right) in enumerate(((5, 19), (6, 20), (1, 3), (2, 4), (0, 0))):
-            for side, u in ((0, to_left), (1, to_right)):
-                sl[side, i, 0:16, :] = coef3[u]
-                sl[side, i, 16:24, :] = source_rows(pa[u * 8 : u * 8 + 8, :])
-        s1[0:16, :] = coef3[0]
-        s1[16:24, :] = source_rows(pa[0:8, :])
-
-    once(sec_pack)
-
+    sq[16:19, :] = pa[21 * 8 : 21 * 8 + 3, :]
     rq[seat] = sq[...]
     group_copies = [
         pltpu.make_async_remote_copy(
@@ -251,6 +238,16 @@
     ]
     for c in group_copies:
         c.start()
+    def sec_pack():
+        for i, (to_left, to_right) in enumerate(((5, 19), (6, 20), (1, 3), (2, 4), (0, 0))):
+            for side, u in ((0, to_left), (1, to_right)):
+                sl[side, i, 0:16, :] = coef3[u]
+                sl[side, i, 16:24, :] = source_rows(pa[u * 8 : u * 8 + 8, :])
+        s1[0:16, :] = coef3[0]
+        s1[16:24, :] = source_rows(pa[0:8, :])
+
+    once(sec_pack)
+
     level_copies = [
         remote(sl.at[0], rlr.at[1], 2, left),
         remote(sl.at[1], rlr.at[0], 3, right),

time: 24.7 us -> 24.5 us (level)
  no operation moved by 1% of the time
where the time goes in v6:
time: 24.5 us; the launch traced here: 24.3 us
  Pallas kernels  22.7 us (93%)
  local copies, waits for them, and re-layouts  1.67 us (7%)
    pallas_call x1, Pallas kernels, body(): pl.pallas_call(functools.partial(kernel, n_dev), out_shape=jax.ShapeDtype...  22.7 us
    unnamed x1, local copies, waits for them, and re-layouts  1.67 us

profile of v6, /device:TPU:0, one launch (start us, length us, event | category | flops | bytes accessed | tf_op | source)
XLA Modules:
  0.0 24.3 jit_solution(14961815524083848496)
XLA Ops:
  0.0 22.7 %hmatvec.1 = f32[16,4096]{1,0:T(8,128)} custom-call(f32[3,4096]{1,0:T(4,128)} %pts_hbm.1, f32[16,4096]{1,0:T(8,128)} %rhs_hbm.1, f32[32,4096]{1,0:T(8,128)} %basis_hbm.1, f32[32,32,84]{2,1,0:T(8,128)} %tr_hbm.1, f32[3,32,85]{2,1,0:T(8,128)} %px_hbm.1, s32[5,64]{1,0:T(8,128)} %bitcast.3, s32[20,84]{1,0:T(8,128)} %bitcast.2, s32[1,128]{1,0:T(1,128)} %rl_hbm.1), custom_call_target="tpu_custom_call" | custom-call | tf_op jit(solution)/shard_map/hmatvec/pallas_call | solution.py:525
  22.7 1.7 %copy.10 = f32[16,4096]{1,0:T(8,128)} copy(f32[16,4096]{1,0:T(8,128)} %hmatvec.1) | data formatting | bytes 524288

commit v7 on v6

--- a/solution.py
+++ b/solution.py
@@ -203,7 +203,7 @@
         tbl[i] = lo
         return c
 
-    lax.fori_loop(0, 21, part, 0, unroll=3)
+    lax.fori_loop(0, 21, part, 0, unroll=7)
 
     def sec_up():
         def rise(first, to):
@@ -328,7 +328,7 @@
         nr[:, pl.ds(pl.multiple_of(v * 256, 256), 256)] = y
         return c
 
-    lax.fori_loop(1, 7, near_unit, 0, unroll=3)
+    lax.fori_loop(1, 7, near_unit, 0, unroll=6)
 
     for o in range(7):
         group_copies[o].wait_send()

time: 24.5 us -> 24.5 us (level)
  no operation moved by 1% of the time
where the time goes in v7:
time: 24.5 us; the launch traced here: 24.3 us
  Pallas kernels  22.6 us (92%)
  local copies, waits for them, and re-layouts  1.67 us (7%)
    pallas_call x1, Pallas kernels, body(): pl.pallas_call(functools.partial(kernel, n_dev), out_shape=jax.ShapeDtype...  22.6 us
    unnamed x1, local copies, waits for them, and re-layouts  1.67 us

profile of v7, /device:TPU:0, one launch (start us, length us, event | category | flops | bytes accessed | tf_op | source)
XLA Modules:
  0.0 24.3 jit_solution(18085144079161605073)
XLA Ops:
  0.0 22.6 %hmatvec.1 = f32[16,4096]{1,0:T(8,128)} custom-call(f32[3,4096]{1,0:T(4,128)} %pts_hbm.1, f32[16,4096]{1,0:T(8,128)} %rhs_hbm.1, f32[32,4096]{1,0:T(8,128)} %basis_hbm.1, f32[32,32,84]{2,1,0:T(8,128)} %tr_hbm.1, f32[3,32,85]{2,1,0:T(8,128)} %px_hbm.1, s32[5,64]{1,0:T(8,128)} %bitcast.3, s32[20,84]{1,0:T(8,128)} %bitcast.2, s32[1,128]{1,0:T(1,128)} %rl_hbm.1), custom_call_target="tpu_custom_call" | custom-call | tf_op jit(solution)/shard_map/hmatvec/pallas_call | solution.py:525
  22.7 1.7 %copy.10 = f32[16,4096]{1,0:T(8,128)} copy(f32[16,4096]{1,0:T(8,128)} %hmatvec.1) | data formatting | bytes 524288
